TPU v7x, 256 devices: a whole 4x4x8 slice. The times are simulated.
256 devices in a mesh: smp: 4 (over z_lo), qry: 32 (over y, z_hi, x), key: 2 (over core).
Axes of the slice: x: 4, y: 4, z: 8 (z_hi: 2, z_lo: 4; z = z_hi * 4 + z_lo), core: 2. Of those that a mesh axis runs over, the one named last changes fastest.
Arguments:
- query_proj: bfloat16 [2048, 8, 768], P('qry', 'smp', 'key'), may hold values from -6 to 6
- key_proj: bfloat16 [2048, 8, 768], P('qry', 'smp', 'key'), may hold values from -6 to 6
- value_proj: bfloat16 [2048, 8, 768], P('qry', 'smp', 'key'), may hold values from -6 to 6
- grad_out: bfloat16 [2048, 8, 768], P('qry', 'smp', 'key'), may hold values from -24 to 24
- pair_feats: bfloat16 [2048, 2048, 128], P('qry', ('smp', 'key')), may hold values from -400 to 400
- pair_gain: float32 [128], replicated, may hold values from 0.1 to 1.9
- bias_weight: bfloat16 [128, 16], replicated, may hold values from -0.5 to 0.5
- atom_counts: int32 [2048], replicated, may hold values from 0 to 23, as said below
Outputs:
- query_grad: bfloat16 [2048, 8, 768], P('qry', 'smp', 'key')
- key_grad: bfloat16 [2048, 8, 768], P('qry', 'smp', 'key')
- value_grad: bfloat16 [2048, 8, 768], P('qry', 'smp', 'key')
- weight_grad: float32 [128, 16], replicated
- gain_grad: float32 [128], replicated
Inputs may be any that keep to these rules, and one draw needn't show every extreme that they name: `atom_counts`: tokens without atoms are padding and form a suffix of 256 to 512 tokens.
All inputs are finite; a program needn't handle non-finite values.
Results may differ from a plain program's by a relative error of at most 0.015.
Values may be sent and summed in bfloat16 or wider, within the bound.
A program may use at most 128 MiB of HBM per device.

v0:
```python
import jax
import jax.numpy as jnp
from jax import lax
from jax.sharding import PartitionSpec as P

DH = 48


def layer_normed(tile_rows):
    values = tile_rows.astype(jnp.float32)
    center = values - jnp.mean(values, axis=-1, keepdims=True)
    spread = jnp.mean(center * center, axis=-1, keepdims=True)
    return center * lax.rsqrt(spread + 1e-05)


def head_bias(normed, pair_gain, bias_weight):
    scaled = normed * pair_gain
    return jnp.einsum(
        "rjc,ch->hrj", scaled, bias_weight.astype(jnp.float32), precision=lax.Precision.HIGHEST
    ).astype(jnp.bfloat16)


def local(
    query_proj, key_proj, value_proj, grad_out, pair_feats, pair_gain, bias_weight, atom_counts
):
    row_count, sample_count, half_width = query_proj.shape
    heads_here = half_width // DH
    factor = DH ** (-0.5)
    normed = layer_normed(pair_feats)
    bias_own = head_bias(normed, pair_gain, bias_weight)
    bias_every = lax.all_gather(bias_own, ("smp", "key"), axis=2, tiled=True)
    bias_heads = lax.dynamic_slice_in_dim(
        bias_every, lax.axis_index("key") * heads_here, heads_here, 0
    )
    keys_all, values_all = (
        lax.all_gather(key_proj, "qry", axis=0, tiled=True),
        lax.all_gather(value_proj, "qry", axis=0, tiled=True),
    )
    token_total = keys_all.shape[0]
    queries = query_proj.reshape(row_count, sample_count, heads_here, DH)
    grads_four = grad_out.reshape(row_count, sample_count, heads_here, DH)
    keys_four = keys_all.reshape(token_total, sample_count, heads_here, DH)
    values_four = values_all.reshape(token_total, sample_count, heads_here, DH)
    scores = (
        jnp.einsum("rshd,kshd->shrk", queries, keys_four, preferred_element_type=jnp.float32)
        * factor
    )
    scores = scores + bias_heads.astype(jnp.float32)[None]
    usable = atom_counts > 0
    scores = jnp.where(usable, scores, -jnp.inf)
    highest_score = jnp.max(scores, axis=-1, keepdims=True)
    exponent = jnp.exp(scores - highest_score)
    total = jnp.sum(exponent, axis=-1, keepdims=True)
    weights = exponent / total
    weights_low = weights.astype(jnp.bfloat16)
    slopes = jnp.einsum(
        "rshd,kshd->shrk", grads_four, values_four, preferred_element_type=jnp.float32
    )
    centred = jnp.sum(weights * slopes, axis=-1, keepdims=True)
    score_grad = weights * (slopes - centred)
    score_low = score_grad.astype(jnp.bfloat16)
    row_total = row_count * lax.axis_size("qry")
    block = weights_low
    product = jnp.einsum("shrk,rshd->kshd", block, grads_four, preferred_element_type=jnp.float32)
    block = score_low
    key_product = jnp.einsum("shrk,rshd->kshd", block, queries, preferred_element_type=jnp.float32)
    combined = lax.psum_scatter(
        jnp.concatenate(
            [
                key_product.reshape(row_total, sample_count, half_width) * factor,
                product.reshape(row_total, sample_count, half_width),
            ],
            axis=2,
        ),
        "qry",
        scatter_dimension=0,
        tiled=True,
    )
    key_sum = combined[:, :, :half_width]
    value_sum = combined[:, :, half_width:]
    query_grad = (
        jnp.einsum("shrk,kshd->rshd", score_low, keys_four, preferred_element_type=jnp.float32)
        * factor
    )
    query_grad = query_grad.astype(jnp.bfloat16).reshape(row_count, sample_count, half_width)
    bias_grad = jnp.sum(score_grad, axis=0)
    group_grad = lax.psum_scatter(
        bias_grad.astype(jnp.bfloat16), "smp", scatter_dimension=2, tiled=True
    ).astype(jnp.float32)
    tiles_grad = lax.all_to_all(group_grad, "key", split_axis=2, concat_axis=0, tiled=True)
    partial_sum = jnp.einsum("rjc,hrj->ch", normed, tiles_grad, precision=lax.Precision.HIGHEST)
    summed = lax.psum(partial_sum, ("smp", "qry", "key"))
    weight_grad = pair_gain[:, None] * summed
    gain_grad = jnp.sum(summed * bias_weight.astype(jnp.float32), axis=1)
    return (
        query_grad,
        key_sum.astype(jnp.bfloat16),
        value_sum.astype(jnp.bfloat16),
        weight_grad,
        gain_grad,
    )


def solution(mesh):
    return jax.shard_map(
        local,
        mesh=mesh,
        in_specs=(
            P("qry", "smp", "key"),
            P("qry", "smp", "key"),
            P("qry", "smp", "key"),
            P("qry", "smp", "key"),
            P("qry", ("smp", "key"), None),
            P(),
            P(),
            P(),
        ),
        out_specs=(
            P("qry", "smp", "key"),
            P("qry", "smp", "key"),
            P("qry", "smp", "key"),
            P(),
            P(),
        ),
        check_vma=False,
    )
```

profile of v0, /device:TPU:1, one launch (start us, length us, event | category | flops | bytes accessed | tf_op | source)
XLA Modules:
  0.0 1050.0 jit_solution(8527724429199901019)
XLA Ops:
  7.2 0.0 copy-start.7
  7.2 0.0 copy-start.8
  7.2 0.0 all-gather.4.cloned.1.call-start
  7.2 0.7 all-gather.4.cloned.1.call-update
  7.9 0.0 all-gather.8.cloned.1.call-start
  8.0 0.7 all-gather.8.cloned.1.call-update
  8.7 0.0 all-gather.6.cloned.1.call-start
  8.7 0.0 copy-start.1
  8.7 3.5 convert_reduce_fusion
  12.3 0.0 copy-done.1
  12.3 0.0 copy-start.4
  12.3 0.0 copy-start.5
  12.3 0.0 copy-start.9
  12.3 0.0 copy-start.6
  12.3 4.7 fusion.8
  17.1 0.0 copy-done.7
  17.1 0.0 copy-done.8
  17.1 8.7 fusion.26
  25.8 0.0 all-gather.6.cloned.1.call-update
  25.8 0.2 reduce-scatter.2.cloned.1.call-start
  26.1 0.0 copy-done.4
  26.1 0.2 copy.70
  26.3 0.0 copy-done.5
  26.3 0.8 copy.71
  27.1 0.0 copy-done.9
  27.1 0.6 dynamic-slice
  28.4 0.0 copy-done.6
  28.4 86.5 %all-gather.4.cloned.1.call-done = bf16[2048,2,384]{2,1,0:T(2,128)(2,1)} async-done(((bf16[64,2,384]{2,1,0:T(2,128)(2,1)}), bf16[2048,2,384]{2,1,0:T(2,128)(2,1)}) %all-gather.4.cloned.1.call-update) | async-done | bytes 3145744 | tf_op jit(solution)/shard_map/all_gather | solution.py:36
  114.9 7.0 copy.51
  121.9 91.4 %all-gather.8.cloned.1.call-done = bf16[2048,2,384]{2,1,0:T(2,128)(2,1)} async-done(((bf16[64,2,384]{2,1,0:T(2,128)(2,1)}), bf16[2048,2,384]{2,1,0:T(2,128)(2,1)}) %all-gather.8.cloned.1.call-update) | async-done | bytes 3145744 | tf_op jit(solution)/shard_map/all_gather | solution.py:37
  213.4 8.7 copy.55
  222.0 43.2 %all-gather.6.cloned.1.call-done = bf16[16,64,2048]{2,0,1:T(8,128)(2,1)} async-done(((bf16[16,64,256]{2,0,1:T(8,128)(2,1)}), bf16[16,64,2048]{2,0,1:T(8,128)(2,1)}) %all-gather.6.cloned.1.call-update) | async-done | bytes 4194320 | tf_op jit(solution)/shard_map/all_gather | solution.py:31
  265.2 2.1 dynamic-slice_convert_fusion
  267.3 4.4 copy.53
  271.7 6.7 fusion.41
  278.3 0.0 copy-start
  278.3 0.0 copy-start.2
  278.3 0.0 copy-start.3
  278.4 7.9 fusion.10
  286.2 0.0 copy-done
  286.2 1.1 copy-done.2
  287.4 0.0 copy-done.3
  287.4 4.0 multiply_reduce_fusion
  291.4 10.3 copy.60
  301.7 10.6 %fusion.21 = (bf16[8,64,2048]{2,1,0:T(8,128)(2,1)}, bf16[2,8,64,2048]{3,2,1,0:T(8,128)(2,1)}) fusion(f32[2,8,64,2048]{3,2,1,0:T(8,128)} %get-tuple-element.34, f32[2,8,64]{2,1,0:T(8,128)S(1)} %get-tuple-element.33, f32[2,8,64,2048]{3,2,1,0:T(8,128)} %get-tuple-element.32, f32[2,8,64]{2,1,0:T(8,128)S(1)} %get-tuple-element.31), kind=kLoop, calls=%fused_computation.28 | loop fusion | flops 9437184 | bytes 23076864 | tf_op jit(solution)/shard_map/reduce_sum | solution.py:86
  312.3 0.0 reduce-scatter.2.cloned.1.call-update
  312.3 5.8 convolution_multiply_fusion
  318.2 10.5 copy.59
  328.6 11.4 %pad_maximum_fusion = f32[2048,2,768]{2,1,0:T(2,128)} fusion(f32[2048,2,384]{2,1,0:T(2,128)} %copy.60, f32[2048,2,384]{2,1,0:T(2,128)} %copy.59), kind=kLoop, calls=%fused_computation.1 | loop fusion | flops 3145728 | bytes 25165824 | tf_op jit(solution)/shard_map/concatenate | solution.py:68
  340.0 588.0 %all-reduce.2 = bf16[2048,2,768]{2,1,0:T(2,128)(2,1)} all-reduce(f32[2048,2,768]{2,1,0:T(2,128)} %pad_maximum_fusion), channel_id=2, replica_groups=mesh['smp'=4,'qry'=32,'key'=2] {'qry'}, use_global_device_ids=true, to_apply=%region_5.6.clone | all-reduce | flops 3145728 | bytes 18874368
  928.0 3.4 fusion.29
  931.4 0.8 copy.64
  932.2 1.1 dynamic-slice_convert_fusion.1
  933.3 0.8 fusion.40
  934.1 1.8 copy.61
  935.9 1.3 reshape.60
  937.3 4.7 all_to_all.18
  941.9 0.5 broadcast.35
  942.4 4.0 reduce
  946.4 1.2 reshape.61
  947.6 1.0 copy.65
  948.7 9.6 fusion.30
  958.3 84.0 %psum.7 = f32[128,16]{0,1:T(8,128)S(1)} all-reduce(f32[128,16]{0,1:T(8,128)S(1)} %fusion.30), channel_id=1, replica_groups=mesh['smp'=4,'qry'=32,'key'=2] {'smp','qry','key'}, use_global_device_ids=true, to_apply=%region_8.9 | all-reduce | flops 2048 | bytes 16384 | tf_op jit(solution)/shard_map/psum | solution.py:92
  1042.3 1.1 multiply_reduce_fusion.1
  (4 shorter events, 0.0 us)
Async XLA Ops:
  7.2 9.9 copy-start.7
  7.2 9.9 copy-start.8
  7.2 107.7 %all-gather.4.cloned.1.call-start = ((), (), s32[]{:S(2)}) async-start(), calls=%async_computation.2 | async-start | bytes 3244032 | tf_op jit(solution)/shard_map/all_gather | solution.py:36
  7.9 205.4 %all-gather.8.cloned.1.call-start = ((), (), s32[]{:S(2)}) async-start(), calls=%async_computation.4 | async-start | bytes 3244032 | tf_op jit(solution)/shard_map/all_gather | solution.py:37
  8.7 256.5 %all-gather.6.cloned.1.call-start = ((), (), s32[]{:S(2)}) async-start(), calls=%async_computation.3 | async-start | bytes 4718592 | tf_op jit(solution)/shard_map/all_gather | solution.py:31
  8.7 3.5 copy-start.1
  12.3 13.8 %copy-start.4 = (bf16[64,2,384]{2,1,0:T(2,128)(2,1)S(1)}, bf16[64,2,384]{2,1,0:T(2,128)(2,1)}, u32[]{:S(2)}) copy-start(bf16[64,2,384]{2,1,0:T(2,128)(2,1)} %param.8) | copy-start | bytes 294916
  12.3 14.0 %copy-start.5 = (bf16[64,2,384]{2,1,0:T(2,128)(2,1)S(1)}, bf16[64,2,384]{2,1,0:T(2,128)(2,1)}, u32[]{:S(2)}) copy-start(bf16[64,2,384]{2,1,0:T(2,128)(2,1)} %param.11) | copy-start | bytes 294916
  12.3 14.9 %copy-start.9 = (u32[256]{0:T(256)S(1)}, u32[256]{0:T(256)}, u32[]{:S(2)}) copy-start(u32[256]{0:T(256)} %constant.31) | copy-start | bytes 3076
  12.3 16.1 %copy-start.6 = (s32[2048]{0:T(1024)S(1)}, s32[2048]{0:T(1024)}, u32[]{:S(2)}) copy-start(s32[2048]{0:T(1024)} %param.15) | copy-start | bytes 24580
  25.8 908.3 %reduce-scatter.2.cloned.1.call-start = ((), (), s32[]{:S(2)}) async-start(), calls=%async_computation.5 | async-start | bytes 2621440 | tf_op jit(solution)/shard_map/reduce_scatter | solution.py:87
  278.3 7.9 copy-start
  278.3 9.0 copy-start.2
  278.3 9.0 copy-start.3
Sparse Core Ops, SparseCore 0:
  11.4 103.4 all-gather.3
  118.3 94.9 all-gather.7
  215.1 50.0 all-gather.5
  312.4 54.7 reduce-scatter.1
where the time goes:
time: 1050 us
  blocking collectives  677 us (64%)
  waiting for transfers between devices  223 us (21%)
  local copies, waits for them, and re-layouts  52.1 us (5%)
  matrix products  46.2 us (4%)
  other arithmetic  37.5 us (4%)
  between operations  14.6 us (1%)
    unnamed x1, blocking collectives  588 us
    all_gather x1, waiting for transfers between devices, local(): lax.all_gather(value_proj, 'qry', axis=0, tiled=True)  91.4 us
    all_gather x1, waiting for transfers between devices, local(): lax.all_gather(key_proj, 'qry', axis=0, tiled=True)  86.5 us
    psum x1, blocking collectives, local(): summed = lax.psum(partial_sum, ('smp', 'qry', 'key'))  84 us
    all_gather x1, waiting for transfers between devices, local(): bias_every = lax.all_gather(bias_own, ('smp', 'key'), axis=2, tiled=True)  43.2 us
  transfers between devices with their start and end apart: 4, of which 3 were waited for; matrix products, arithmetic and copies ran while one was open for 6% of the time, Pallas kernels for 0%

commit v1 on v0

v1 whole, which is shorter than its diff:
```python
import jax
import jax.numpy as jnp
from jax import lax
from jax.experimental import pallas as pl
from jax.experimental.pallas import tpu as pltpu
from jax.sharding import PartitionSpec as P

DH = 48
HEADS = 16
TOKENS = 2048
LIVE = 1792
ROWS = 128
CHUNKS = 4
PAIRS = 14
FACTOR = DH ** (-0.5)
LOG2E = 1.4426950408889634
MESH = pl.DeviceIdType.MESH
F32 = jnp.float32
BF16 = jnp.bfloat16


def rem(a, b):
    return lax.rem(a, jnp.int32(b))


def div(a, b):
    return lax.div(a, jnp.int32(b))


def dot(a, b):
    return jnp.dot(a, b, preferred_element_type=F32)


def dot_nt(a, b):
    return lax.dot_general(a, b, (((1,), (1,)), ((), ())), preferred_element_type=F32)


def wait_bytes(ref, sem):
    pltpu.make_async_copy(ref, ref, sem).wait()


def kernel(
    a_ref, x_ref, wt_ref, gain_ref, ac_ref,
    o_ref, wg_ref, gg_ref,
    n_ref, skv, sqd, g_ref, r_ref, bsf, bs, br, bf,
    kvt, qdt, s_ref, p_ref, w_ref, ds_ref, db, dkv, dq, d_ref, qb,
    h1, f1, h2, f2, fb, ob, dbs, dr, df, ra, rb,
    x_sem, kv_send, kv_recv, qd_sem, bias_sem, ag_send, ag_recv,
    rs_send, rs_recv, ob_sem, db_sem, ar_sem,
):
    smp = lax.axis_index("smp")
    qry = lax.axis_index("qry")
    key = lax.axis_index("key")
    y = div(qry, 8)
    zh = rem(div(qry, 4), 2)
    x = rem(qry, 4)
    z = zh * 4 + smp
    cidx = smp * 2 + key
    head = key * 8 + z
    live_cols = cidx < 7

    def dev(xx, yy, zz, kk):
        return (rem(zz, 4), yy * 8 + div(zz, 4) * 4 + xx, kk)

    def rcopy(src, dst, send, recv, device):
        return pltpu.make_async_remote_copy(
            src_ref=src, dst_ref=dst, send_sem=send, recv_sem=recv, device_id=device, device_id_type=MESH
        )

    def zline():
        for dz in range(8):
            for dk in range(2):
                yield dz, dk, rem(z + dz, 8), rem(key + dk, 2)

    x_copies = [
        pltpu.make_async_copy(x_ref.at[pl.ds(16 * rc, 16)], n_ref.at[pl.ds(16 * rc, 16)], x_sem.at[rc])
        for rc in range(4)
    ]
    for copy in x_copies:
        copy.start()

    barrier = pltpu.get_barrier_semaphore()
    for dz, dk, zz, kk in zline():
        if dz or dk:
            pl.semaphore_signal(barrier, inc=1, device_id=dev(x, y, zz, kk), device_id_type=MESH)
    for dy in range(4):
        for dx in range(4):
            if dy or dx:
                pl.semaphore_signal(
                    barrier, inc=1, device_id=dev(rem(x + dx, 4), rem(y + dy, 4), z, key), device_id_type=MESH
                )

    for a in range(4):
        turned = a_ref[a].astype(F32).T.astype(BF16).reshape(8, DH, 128)
        if a < 2:
            skv[:, a] = turned
        else:
            sqd[:, a - 2] = turned

    db[...] = jnp.zeros_like(db)
    for c in range(CHUNKS):
        d_ref[c, 3, :, 1] = jnp.zeros((4, 2, DH, 128), BF16)

    pl.semaphore_wait(barrier, 30)

    for dz in range(8):
        zz = rem(z + dz, 8)
        dst = g_ref.at[smp, y, x, zh]
        if dz == 0:
            pltpu.make_async_copy(skv.at[zz], dst, kv_recv.at[smp]).start()
        else:
            rcopy(skv.at[zz], dst, kv_send, kv_recv.at[smp], dev(x, y, zz, key)).start()
    for dz in range(8):
        zz = rem(z + dz, 8)
        dst = r_ref.at[smp, zh]
        if dz == 0:
            pltpu.make_async_copy(sqd.at[zz], dst, qd_sem.at[1]).start()
        else:
            rcopy(sqd.at[zz], dst, qd_sem.at[0], qd_sem.at[1], dev(x, y, zz, key)).start()

    gw = wt_ref[...] * gain_ref[...]
    gw_high = gw.astype(BF16)
    gw_low = (gw - gw_high.astype(F32)).astype(BF16)
    gw_both = jnp.concatenate([gw_high, gw_low], axis=0)
    mean_of = jnp.full((128, 128), 1.0 / 128, BF16)

    def bias_rows(rc):
        x_copies[rc].wait()

        def step(i, carry):
            row = rc * 16 + 2 * i
            tile = n_ref[pl.ds(row, 2)].reshape(512, 128)
            center = tile.astype(F32) - dot(tile, mean_of)
            square = center * center
            high = square.astype(BF16)
            low = (square - high.astype(F32)).astype(BF16)
            spread = dot(high, mean_of) + dot(low, mean_of)
            normed = (center * lax.rsqrt(spread + 1e-05)).astype(BF16)
            n_ref[pl.ds(row, 2)] = normed.reshape(2, 256, 128)
            out = dot_nt(gw_both, normed)
            out = out[:16] + out[16:]
            for j in range(2):
                for half in range(2):
                    bsf[half, pl.ds((2 * i + j) * 16, 16)] = out[:, j * 256 + half * 128 : j * 256 + half * 128 + 128]
            return carry

        lax.fori_loop(0, 8, step, 0)
        for h in range(16):
            pieces = [bsf[half, pl.ds(h, 16, stride=16)] for half in range(2)]
            bs[rc, h] = jnp.concatenate(pieces, axis=1).astype(BF16)

        @pl.when(live_cols)
        def _():
            dst = br.at[pl.ds(zh * 64 + 16 * rc, 16), pl.ds(pl.multiple_of(cidx * 256, 256), 256)]
            for dz, dk, zz, kk in zline():
                src = bs.at[rc, kk * 8 + zz]
                if dz or dk:
                    rcopy(src, dst, bias_sem.at[0], bias_sem.at[1], dev(x, y, zz, kk)).start()
                else:
                    pltpu.make_async_copy(src, dst, bias_sem.at[1]).start()

    def spot(c, dp, dq):
        dx, dy = (dp, dq) if c % 2 == 0 else (dq, dp)
        return rem(x + dx + 4, 4), rem(y + dy + 4, 4)

    def there(c, dp, dq):
        xx, yy = spot(c, dp, dq)
        return dev(xx, yy, z, key)

    def block(c, dp, dq):
        xx, yy = spot(c, dp, dq)
        return (c, yy, xx)

    def gather_send(c, where, half, sem, target):
        src = g_ref.at[where] if half is None else g_ref.at[where + (half,)]
        rcopy(src, src, ag_send.at[c, sem], ag_recv.at[where + (half or 0,)], target).start()

    def gather_wait(where, half):
        ref = g_ref.at[where] if half is None else g_ref.at[where + (half,)]
        wait_bytes(ref, ag_recv.at[where + (half or 0,)])

    def gather_1(c):
        wait_bytes(g_ref.at[c, y, x], kv_recv.at[c])
        for d in (1, -1):
            gather_send(c, block(c, 0, 0), None, 0, there(c, d, 0))

    def gather_2(c):
        for d in (1, -1):
            gather_send(c, block(c, 0, 0), None, 1, there(c, 0, d))
        for half, d in ((0, 1), (1, -1)):
            where = block(c, -d, 0)
            gather_wait(where, None)
            gather_send(c, where, half, 3, there(c, d, 0))
            for e in (1, -1):
                gather_send(c, where, None, 1, there(c, 0, e))

    def gather_3(c):
        where = block(c, 2, 0)
        for half in range(2):
            gather_wait(where, half)
        for e in (1, -1):
            gather_send(c, where, None, 0, there(c, 0, e))

    def gather_4(c):
        for dp in (0, -1, 1, 2):
            for half, e in ((0, 1), (1, -1)):
                where = block(c, dp, -e)
                gather_wait(where, None)
                gather_send(c, where, half, 2, there(c, 0, e))

    def gather_5(c):
        for dp in (0, -1, 1, 2):
            for half in range(2):
                gather_wait(block(c, dp, 2), half)

    def gather_end(c):
        wait_bytes(g_ref.at[c, 0], ag_send.at[c, 0])
        wait_bytes(g_ref.at[c, pl.ds(0, 3), pl.ds(0, 2)], ag_send.at[c, 1])
        wait_bytes(g_ref.at[c, 0], ag_send.at[c, 2])
        wait_bytes(g_ref.at[c, 0, 0], ag_send.at[c, 3])

    low_lanes = lax.broadcasted_iota(jnp.int32, (DH, 128), 1) < 64

    def merge(first, second):
        return (
            jnp.where(low_lanes, first, pltpu.roll(second, 64, 1)),
            jnp.where(low_lanes, pltpu.roll(first, 64, 1), second),
        )

    def attention(c):
        for yy in range(4):
            for hi in range(2):
                if yy == 3 and hi == 1:
                    continue
                for m in range(2):
                    tile = yy * 4 + hi * 2 + m
                    for a in range(2):
                        both = merge(
                            g_ref[c, yy, 2 * m, hi, a].astype(F32), g_ref[c, yy, 2 * m + 1, hi, a].astype(F32)
                        )
                        for par in range(2):
                            kvt[par, a, :, tile * 128 : tile * 128 + 128] = both[par].astype(BF16)
        for a in range(2):
            both = merge(r_ref[c, 0, a].astype(F32), r_ref[c, 1, a].astype(F32))
            for par in range(2):
                qdt[par, a] = both[par].astype(BF16)

        def one(par, carry):
            query_t, grad_t = qdt[par, 0], qdt[par, 1]
            query = query_t.astype(F32).T.astype(BF16)
            grad = grad_t.astype(F32).T.astype(BF16)
            keys_t, values_t = kvt[par, 0], kvt[par, 1]
            s_ref[...] = dot(query, keys_t)
            p_ref[...] = dot(grad, values_t)

            def rows(g, inner):
                at = pl.ds(pl.multiple_of(g * 16, 16), 16)
                scores = s_ref[at] * (FACTOR * LOG2E) + bf[at]
                top = jnp.max(scores, axis=1, keepdims=True)
                exponent = jnp.exp2(scores - top)
                slopes = p_ref[at]
                total = jnp.sum(exponent, axis=1, keepdims=True)
                mixed = jnp.sum(exponent * slopes, axis=1, keepdims=True)
                inverse = 1.0 / total
                weights = exponent * inverse
                score_grad = weights * (slopes - mixed * inverse)
                w_ref[at] = weights.astype(BF16)
                ds_ref[at] = score_grad.astype(BF16)
                db[at] += score_grad
                return inner

            lax.fori_loop(0, 8, rows, 0)
            dkv[par, 0] = dot(query_t, ds_ref[...])
            dkv[par, 1] = dot(grad_t, w_ref[...])
            dq[par] = dot_nt(keys_t, ds_ref[...]) * FACTOR
            return carry

        lax.fori_loop(0, 2, one, 0)
        for yy in range(4):
            for hi in range(2):
                if yy == 3 and hi == 1:
                    continue
                for m in range(2):
                    tile = yy * 4 + hi * 2 + m
                    for a in range(2):
                        lanes = slice(tile * 128, tile * 128 + 128)
                        both = merge(dkv[0, a, :, lanes], dkv[1, a, :, lanes])
                        for e in range(2):
                            d_ref[c, yy, 2 * m + e, hi, a] = both[e].astype(BF16)
        both = merge(dq[0], dq[1])
        for hi in range(2):
            qb[c, hi] = both[hi].astype(BF16)

    def line(c, dp, half=None):
        xx, yy = spot(c, dp, 0)
        ref = d_ref.at[c, :, xx] if c % 2 == 0 else d_ref.at[c, yy]
        return ref if half is None else ref.at[:, half]

    def home(c, dq):
        return d_ref.at[block(c, 0, dq)]

    def plus(ref, *others):
        total = ref[...].astype(F32)
        for other in others:
            total += other[...].astype(F32)
        return total

    def reduce_1(c):
        for half, d in ((0, 1), (1, -1)):
            rcopy(line(c, 2, half), h1.at[c, half], rs_send.at[c, 0], rs_recv.at[c, half], there(c, d, 0)).start()

    def reduce_2(c):
        for half, d in ((0, 1), (1, -1)):
            wait_bytes(h1.at[c, half], rs_recv.at[c, half])
            ref = line(c, d, half)
            ref[...] = plus(ref, h1.at[c, half]).astype(BF16)
            rcopy(line(c, d), f1.at[c, half], rs_send.at[c, 1], rs_recv.at[c, 2 + half], there(c, d, 0)).start()

    def reduce_3(c):
        for half in range(2):
            wait_bytes(f1.at[c, half], rs_recv.at[c, 2 + half])
        ref = line(c, 0)
        ref[...] = plus(ref, f1.at[c, 0], f1.at[c, 1]).astype(BF16)
        for half, e in ((0, 1), (1, -1)):
            rcopy(
                home(c, 2).at[half], h2.at[c, half], rs_send.at[c, 2], rs_recv.at[c, 4 + half], there(c, 0, e)
            ).start()

    def reduce_4(c):
        for half, e in ((0, 1), (1, -1)):
            wait_bytes(h2.at[c, half], rs_recv.at[c, 4 + half])
            ref = home(c, e).at[half]
            ref[...] = plus(ref, h2.at[c, half]).astype(BF16)
            rcopy(home(c, e), f2.at[c, half], rs_send.at[c, 3], rs_recv.at[c, 6 + half], there(c, 0, e)).start()

    def back(src, c, hi, lo, count):
        zz = jnp.int32(4 * hi + c)
        dst = ob.at[z, pl.ds(lo, count)]

        @pl.when(zz == z)
        def _():
            pltpu.make_async_copy(src, dst, ob_sem.at[1]).start()

        @pl.when(zz != z)
        def _():
            rcopy(src, dst, ob_sem.at[0], ob_sem.at[1], dev(x, y, zz, key)).start()

    def reduce_5(c):
        for half in range(2):
            wait_bytes(f2.at[c, half], rs_recv.at[c, 6 + half])
        ref = home(c, 0)
        for hi in range(2):
            for a in range(2):
                total = plus(ref.at[hi, a], f2.at[c, 0, hi, a], f2.at[c, 1, hi, a])
                fb[c, hi, a] = (total * FACTOR if a == 0 else total).astype(BF16)
            back(fb.at[c, hi], c, hi, 0, 2)

    def query_back(c):
        for hi in range(2):
            back(qb.at[c, pl.ds(hi, 1)], c, hi, 2, 1)

    def reduce_end(c):
        for i, ref in enumerate((h1, f1, h2, f2)):
            wait_bytes(ref.at[c], rs_send.at[c, i])

    bias_rows(0)
    for c in range(CHUNKS):
        gather_1(c)
    bias_rows(1)
    for c in range(CHUNKS):
        gather_2(c)
    bias_rows(2)
    for c in range(CHUNKS):
        gather_3(c)
    bias_rows(3)
    for c in range(CHUNKS):
        gather_4(c)

    wait_bytes(r_ref, qd_sem.at[1])
    wait_bytes(br, bias_sem.at[1])
    mask = jnp.where(ac_ref[...] > 0, 0.0, -jnp.inf).astype(F32)

    def widen(g, carry):
        at = pl.ds(pl.multiple_of(g * 16, 16), 16)
        bf[at] = (br[at].astype(F32) + mask[:, :LIVE]) * LOG2E
        return carry

    lax.fori_loop(0, 8, widen, 0)

    gather_5(0)
    attention(0)
    reduce_1(0)
    query_back(0)
    gather_5(1)
    attention(1)
    reduce_1(1)
    reduce_2(0)
    query_back(1)
    gather_5(2)
    attention(2)
    reduce_1(2)
    reduce_2(1)
    reduce_3(0)
    query_back(2)
    gather_5(3)
    attention(3)
    reduce_1(3)

    for hi in range(2):
        for col in range(7):
            dbs[hi * 8 + col] = db[hi * 64 : hi * 64 + 64, col * 256 : col * 256 + 256].astype(BF16)
    for dz, dk, zz, kk in zline():
        target = rem(zz, 4) * 2 + kk
        src = dbs.at[div(zz, 4) * 8 + target]
        dst = dr.at[head]

        @pl.when(target < 7)
        def _():
            if dz or dk:
                rcopy(src, dst, db_sem.at[0], db_sem.at[1], dev(x, y, zz, kk)).start()
            else:
                pltpu.make_async_copy(src, dst, db_sem.at[1]).start()

    query_back(3)
    reduce_2(2)
    reduce_3(1)
    reduce_4(0)
    reduce_2(3)
    reduce_3(2)
    reduce_4(1)
    reduce_5(0)
    reduce_3(3)
    reduce_4(2)
    reduce_5(1)
    reduce_4(3)
    reduce_5(2)

    @pl.when(live_cols)
    def _():
        wait_bytes(dr, db_sem.at[1])
        for h in range(16):
            wide = dr[h].astype(F32)
            for half in range(2):
                df[half, pl.ds(h * 64, 64)] = wide[:, half * 128 : half * 128 + 128]

        def step(r, acc):
            left = jnp.concatenate([df[half, pl.ds(r, 16, stride=64)] for half in range(2)], axis=1)
            return acc + dot(left.astype(BF16), n_ref[r])

        ra[y * 4 + x] = lax.fori_loop(0, 64, step, jnp.zeros((16, 128), F32))

    @pl.when(cidx == 7)
    def _():
        ra[y * 4 + x] = jnp.zeros((16, 128), F32)

    for dy in range(4):
        for dx in range(4):
            if dy or dx:
                mine = ra.at[y * 4 + x]
                rcopy(mine, mine, ar_sem.at[0], ar_sem.at[1], dev(rem(x + dx, 4), rem(y + dy, 4), z, key)).start()
    reduce_5(3)
    wait_bytes(ra.at[pl.ds(0, 15)], ar_sem.at[1])
    total = ra[0]
    for i in range(1, 16):
        total += ra[i]
    rb[head] = total
    for dz, dk, zz, kk in zline():
        if dz or dk:
            mine = rb.at[head]
            rcopy(mine, mine, ar_sem.at[2], ar_sem.at[3], dev(x, y, zz, kk)).start()

    wait_bytes(ob, ob_sem.at[1])
    for a in range(3):
        o_ref[a] = ob[:, a].reshape(8 * DH, 128).astype(F32).T.astype(BF16)

    wait_bytes(rb.at[pl.ds(0, 15)], ar_sem.at[3])
    summed = rb[0]
    for i in range(1, 16):
        summed += rb[i]
    wg_ref[...] = summed * gain_ref[...]
    gg_ref[...] = jnp.sum(summed * wt_ref[...], axis=0, keepdims=True)

    wait_bytes(skv.at[pl.ds(0, 7)], kv_send)
    wait_bytes(sqd.at[pl.ds(0, 7)], qd_sem.at[0])

    @pl.when(live_cols)
    def _():
        wait_bytes(bs.at[:, pl.ds(0, 15)], bias_sem.at[0])
        wait_bytes(dbs.at[pl.ds(0, 13)], db_sem.at[0])

    @pl.when(cidx == 7)
    def _():
        wait_bytes(dbs.at[pl.ds(0, 14)], db_sem.at[0])

    for c in range(CHUNKS):
        gather_end(c)
        reduce_end(c)
    wait_bytes(ob.at[pl.ds(0, 7)], ob_sem.at[0])
    wait_bytes(ra.at[pl.ds(0, 15)], ar_sem.at[0])
    wait_bytes(rb.at[pl.ds(0, 15)], ar_sem.at[2])


def fused(stacked, pair_feats, weight_t, gain, counts):
    vmem = pl.BlockSpec(memory_space=pltpu.VMEM)
    scratch = [
        pltpu.VMEM((64, 256, 128), BF16),
        pltpu.VMEM((8, 2, DH, 128), BF16),
        pltpu.VMEM((8, 2, DH, 128), BF16),
        pltpu.VMEM((4, 4, 4, 2, 2, DH, 128), BF16),
        pltpu.VMEM((4, 2, 2, DH, 128), BF16),
        pltpu.VMEM((2, 256, 128), F32),
        pltpu.VMEM((4, 16, 16, 256), BF16),
        pltpu.VMEM((ROWS, LIVE), BF16),
        pltpu.VMEM((ROWS, LIVE), F32),
        pltpu.VMEM((2, 2, DH, LIVE), BF16),
        pltpu.VMEM((2, 2, DH, 128), BF16),
        pltpu.VMEM((ROWS, LIVE), F32),
        pltpu.VMEM((ROWS, LIVE), F32),
        pltpu.VMEM((ROWS, LIVE), BF16),
        pltpu.VMEM((ROWS, LIVE), BF16),
        pltpu.VMEM((ROWS, LIVE), F32),
        pltpu.VMEM((2, 2, DH, LIVE), F32),
        pltpu.VMEM((2, DH, 128), F32),
        pltpu.VMEM((4, 4, 4, 2, 2, DH, 128), BF16),
        pltpu.VMEM((4, 2, DH, 128), BF16),
        pltpu.VMEM((4, 2, 4, 2, DH, 128), BF16),
        pltpu.VMEM((4, 2, 4, 2, 2, DH, 128), BF16),
        pltpu.VMEM((4, 2, 2, DH, 128), BF16),
        pltpu.VMEM((4, 2, 2, 2, DH, 128), BF16),
        pltpu.VMEM((4, 2, 2, DH, 128), BF16),
        pltpu.VMEM((8, 3, DH, 128), BF16),
        pltpu.VMEM((16, 64, 256), BF16),
        pltpu.VMEM((16, 64, 256), BF16),
        pltpu.VMEM((2, 1024, 128), F32),
        pltpu.VMEM((16, 16, 128), F32),
        pltpu.VMEM((16, 16, 128), F32),
        pltpu.SemaphoreType.DMA((4,)),
        pltpu.SemaphoreType.DMA,
        pltpu.SemaphoreType.DMA((4,)),
        pltpu.SemaphoreType.DMA((2,)),
        pltpu.SemaphoreType.DMA((2,)),
        pltpu.SemaphoreType.DMA((4, 4)),
        pltpu.SemaphoreType.DMA((4, 4, 4, 2)),
        pltpu.SemaphoreType.DMA((4, 4)),
        pltpu.SemaphoreType.DMA((4, 8)),
        pltpu.SemaphoreType.DMA((2,)),
        pltpu.SemaphoreType.DMA((2,)),
        pltpu.SemaphoreType.DMA((4,)),
    ]
    return pl.pallas_call(
        kernel,
        out_shape=(
            jax.ShapeDtypeStruct((3, 128, 8 * DH), BF16),
            jax.ShapeDtypeStruct((16, 128), F32),
            jax.ShapeDtypeStruct((1, 128), F32),
        ),
        in_specs=[vmem, pl.BlockSpec(memory_space=pl.ANY), vmem, vmem, vmem],
        out_specs=(vmem, vmem, vmem),
        scratch_shapes=scratch,
        compiler_params=pltpu.CompilerParams(
            collective_id=0, has_side_effects=True, vmem_limit_bytes=56 * 1024 * 1024
        ),
    )(stacked, pair_feats, weight_t, gain, counts)


def local(
    query_proj, key_proj, value_proj, grad_out, pair_feats, pair_gain, bias_weight, atom_counts
):
    stacked = jnp.stack([key_proj, value_proj, query_proj, grad_out])
    stacked = stacked.transpose(0, 2, 1, 3).reshape(4, 128, 8 * DH)
    out, weight_t, gain_grad = fused(
        stacked,
        pair_feats,
        bias_weight.astype(F32).T,
        pair_gain[None],
        atom_counts[None],
    )
    out = out.reshape(3, 2, 64, 8 * DH).transpose(0, 2, 1, 3)
    return out[2], out[0], out[1], weight_t.T, gain_grad[0]


def solution(mesh):
    tokens = P("qry", "smp", "key")
    return jax.shard_map(
        local,
        mesh=mesh,
        in_specs=(tokens, tokens, tokens, tokens, P("qry", ("smp", "key"), None), P(), P(), P()),
        out_specs=(tokens, tokens, tokens, P(), P()),
        check_vma=False,
    )
```

time: 1050 us -> 115 us (0.11)
  blocking collectives: 677 us -> 0 us
  waiting for transfers between devices: 223 us -> 0 us
  Pallas kernels: 0 us -> 106 us
  local copies, waits for them, and re-layouts: 52.1 us -> 5.35 us
  matrix products: 46.2 us -> 0 us
  other arithmetic: 37.5 us -> 3.03 us
  between operations: 14.6 us -> 0.65 us
    unnamed x1 -> x0, blocking collectives: 588 us -> none
    all_gather x3 -> x0, waiting for transfers between devices: 221 us -> none  [the longest x1 91.4 us: local(): lax.all_gather(value_proj, 'qry', axis=0, tiled=True)]
    pallas_call x0 -> x1, Pallas kernels: none -> 106 us  [fused(): pl.pallas_call(kernel, out_shape=(jax.ShapeDtypeStruct((3, 128, 8 * DH),...]
    psum x1 -> x0, blocking collectives: 84 us -> none  [local(): summed = lax.psum(partial_sum, ('smp', 'qry', 'key'))]
    dot_general x6 -> x0, matrix products: 39.5 us -> none  [the longest x1 9.64 us: local(): jnp.einsum('rjc,hrj->ch', normed, tiles_grad, precision=lax.Precision.HIG...]
    reduce_sum x4 -> x0, other arithmetic: 20 us -> none  [the longest x1 10.6 us: local(): bias_grad = jnp.sum(score_grad, axis=0)]
    all_gather x2 -> x0, local copies, waits for them, and re-layouts: 15.7 us -> none  [the longest x1 8.65 us: local(): lax.all_gather(value_proj, 'qry', axis=0, tiled=True)]
    concatenate x1 -> x0, other arithmetic: 11.4 us -> none  [local(): jnp.concatenate([key_product.reshape(row_total, sample_count, half_width)...]
  transfers between devices with their start and end apart: 4 -> 0, of which waited for: 3 -> 0; matrix products, arithmetic and copies ran while one was open for 6% -> 0% of each run, Pallas kernels for 0% -> 0%
where the time goes in v1:
time: 115 us
  Pallas kernels  106 us (92%)
  local copies, waits for them, and re-layouts  5.35 us (5%)
  other arithmetic  3.03 us (3%)
    pallas_call x1, Pallas kernels, fused(): pl.pallas_call(kernel, out_shape=(jax.ShapeDtypeStruct((3, 128, 8 * DH),...  106 us
    unnamed x2, local copies, waits for them, and re-layouts  2.41 us

profile of v1, /device:TPU:1, one launch (start us, length us, event | category | flops | bytes accessed | tf_op | source)
XLA Modules:
  0.0 114.6 jit_solution(12110024818520232319)
XLA Ops:
  0.6 1.7 %maximum_bitcast_fusion = bf16[4,2,64,384]{3,1,2,0:T(2,128)(2,1)S(1)} fusion(bf16[1,64,2,384]{3,2,1,0:T(2,128)(2,1)} %bitcast.26, bf16[1,64,2,384]{3,2,1,0:T(2,128)(2,1)} %bitcast.27, bf16[1,64,2,384]{3,2,1,0:T(2,128)(2,1)} %bitcast.28, bf16[1,64,2,384]{3,2,1,0:T(2,128)(2,1)} %bitcast.29), kind=kLoop, calls=%fused_computation | loop fusion | flops 589824 | bytes 786432 | tf_op jit(solution)/shard_map/transpose | solution.py:570
  2.4 0.8 copy.13
  3.2 1.3 %convert_bitcast_fusion.wt_ref = f32[16,128]{1,0:T(8,128)} fusion(bf16[128,16]{0,1:T(8,128)(2,1)} %param.14), kind=kLoop, calls=%fused_computation.5 | loop fusion | flops 2048 | bytes 12288 | tf_op jit(solution)/shard_map/transpose | solution.py:574
  4.5 105.6 %shard_map.119 = (bf16[3,128,384]{2,1,0:T(8,128)(2,1)}, f32[16,128]{1,0:T(8,128)}, f32[1,128]{1,0:T(1,128)}) custom-call(bf16[4,128,384]{2,1,0:T(8,128)(2,1)} %bitcast.23, bf16[64,256,128]{2,1,0:T(8,128)(2,1)} %x_ref.1, f32[16,128]{1,0:T(8,128)} %convert_bitcast_fusion.wt_ref, f32[1,128]{1,0:T(1,128)} %bitcast.32, s32[1,2048]{1,0:T(1,128)} %bitcast.30), custom_call_target="tpu_custom_call" | custom-call | tf_op jit(solution)/shard_map/pallas_call | solution.py:550
  110.1 1.3 %copy.16 = bf16[3,2,64,384]{3,1,2,0:T(2,128)(2,1)S(1)} copy(bf16[3,2,64,384]{3,2,1,0:T(8,128)(2,1)} %bitcast.25) | data formatting | bytes 589824 | tf_op jit(solution)/shard_map/reshape | solution.py:578
  111.3 0.9 slice_bitcast_fusion
  112.2 1.3 %copy.19 = f32[128,16]{0,1:T(8,128)} copy(f32[128,16]{0,1:T(8,128)} %bitcast.31) | data formatting | bytes 16384
  113.5 1.1 copy.20

commit v2 on v1

--- a/solution.py
+++ b/solution.py
@@ -97,28 +97,10 @@
         else:
             sqd[:, a - 2] = turned
 
-    db[...] = jnp.zeros_like(db)
     for c in range(CHUNKS):
         d_ref[c, 3, :, 1] = jnp.zeros((4, 2, DH, 128), BF16)
 
-    pl.semaphore_wait(barrier, 30)
-
-    for dz in range(8):
-        zz = rem(z + dz, 8)
-        dst = g_ref.at[smp, y, x, zh]
-        if dz == 0:
-            pltpu.make_async_copy(skv.at[zz], dst, kv_recv.at[smp]).start()
-        else:
-            rcopy(skv.at[zz], dst, kv_send, kv_recv.at[smp], dev(x, y, zz, key)).start()
-    for dz in range(8):
-        zz = rem(z + dz, 8)
-        dst = r_ref.at[smp, zh]
-        if dz == 0:
-            pltpu.make_async_copy(sqd.at[zz], dst, qd_sem.at[1]).start()
-        else:
-            rcopy(sqd.at[zz], dst, qd_sem.at[0], qd_sem.at[1], dev(x, y, zz, key)).start()
-
-    gw = wt_ref[...] * gain_ref[...]
+    gw = wt_ref[...].astype(F32) * gain_ref[...]
     gw_high = gw.astype(BF16)
     gw_low = (gw - gw_high.astype(F32)).astype(BF16)
     gw_both = jnp.concatenate([gw_high, gw_low], axis=0)
@@ -144,11 +126,12 @@
                     bsf[half, pl.ds((2 * i + j) * 16, 16)] = out[:, j * 256 + half * 128 : j * 256 + half * 128 + 128]
             return carry
 
-        lax.fori_loop(0, 8, step, 0)
+        lax.fori_loop(0, 8, step, 0, unroll=2)
         for h in range(16):
             pieces = [bsf[half, pl.ds(h, 16, stride=16)] for half in range(2)]
             bs[rc, h] = jnp.concatenate(pieces, axis=1).astype(BF16)
 
+    def bias_send(rc):
         @pl.when(live_cols)
         def _():
             dst = br.at[pl.ds(zh * 64 + 16 * rc, 16), pl.ds(pl.multiple_of(cidx * 256, 256), 256)]
@@ -159,6 +142,29 @@
                 else:
                     pltpu.make_async_copy(src, dst, bias_sem.at[1]).start()
 
+    bias_rows(0)
+    pl.semaphore_wait(barrier, 30)
+
+    for dz in range(8):
+        zz = rem(z + dz, 8)
+        dst = g_ref.at[smp, y, x, zh]
+        if dz == 0:
+            pltpu.make_async_copy(skv.at[zz], dst, kv_recv.at[smp]).start()
+        else:
+            rcopy(skv.at[zz], dst, kv_send, kv_recv.at[smp], dev(x, y, zz, key)).start()
+    for dz in range(8):
+        zz = rem(z + dz, 8)
+        dst = r_ref.at[smp, zh]
+        if dz == 0:
+            pltpu.make_async_copy(sqd.at[zz], dst, qd_sem.at[1]).start()
+        else:
+            rcopy(sqd.at[zz], dst, qd_sem.at[0], qd_sem.at[1], dev(x, y, zz, key)).start()
+
+    bias_send(0)
+    for rc in range(1, 4):
+        bias_rows(rc)
+        bias_send(rc)
+
     def spot(c, dp, dq):
         dx, dy = (dp, dq) if c % 2 == 0 else (dq, dp)
         return rem(x + dx + 4, 4), rem(y + dy + 4, 4)
@@ -181,43 +187,40 @@
 
     def gather_1(c):
         wait_bytes(g_ref.at[c, y, x], kv_recv.at[c])
-        for d in (1, -1):
-            gather_send(c, block(c, 0, 0), None, 0, there(c, d, 0))
-
-    def gather_2(c):
-        for d in (1, -1):
-            gather_send(c, block(c, 0, 0), None, 1, there(c, 0, d))
-        for half, d in ((0, 1), (1, -1)):
-            where = block(c, -d, 0)
-            gather_wait(where, None)
-            gather_send(c, where, half, 3, there(c, d, 0))
-            for e in (1, -1):
-                gather_send(c, where, None, 1, there(c, 0, e))
+        for dp in (1, -1, 2):
+            gather_send(c, block(c, 0, 0), None, 0, there(c, dp, 0))
+
+    def gather_2(c, steps):
+        for dp in (0, 1, -1, 2):
+            where = block(c, dp, 0)
+            if dp:
+                gather_wait(where, None)
+            for dq in steps:
+                gather_send(c, where, None, 1, there(c, 0, dq))
 
     def gather_3(c):
-        where = block(c, 2, 0)
-        for half in range(2):
-            gather_wait(where, half)
-        for e in (1, -1):
-            gather_send(c, where, None, 0, there(c, 0, e))
+        for dp in (0, 1, -1, 2):
+            for half, dq in ((0, 1), (1, -1)):
+                where = block(c, dp, -dq)
+                gather_wait(where, None)
+                gather_send(c, where, half, 2, there(c, 0, dq))
 
     def gather_4(c):
-        for dp in (0, -1, 1, 2):
-            for half, e in ((0, 1), (1, -1)):
-                where = block(c, dp, -e)
-                gather_wait(where, None)
-                gather_send(c, where, half, 2, there(c, 0, e))
-
-    def gather_5(c):
-        for dp in (0, -1, 1, 2):
-            for half in range(2):
-                gather_wait(block(c, dp, 2), half)
+        for dp in (0, 1, -1, 2):
+            if c < 2:
+                for half in range(2):
+                    gather_wait(block(c, dp, 2), half)
+            else:
+                for dq in (1, -1, 2):
+                    gather_wait(block(c, dp, dq), None)
 
     def gather_end(c):
-        wait_bytes(g_ref.at[c, 0], ag_send.at[c, 0])
-        wait_bytes(g_ref.at[c, pl.ds(0, 3), pl.ds(0, 2)], ag_send.at[c, 1])
-        wait_bytes(g_ref.at[c, 0], ag_send.at[c, 2])
-        wait_bytes(g_ref.at[c, 0, 0], ag_send.at[c, 3])
+        wait_bytes(g_ref.at[c, 0, pl.ds(0, 3)], ag_send.at[c, 0])
+        if c < 2:
+            wait_bytes(g_ref.at[c, pl.ds(0, 2)], ag_send.at[c, 1])
+            wait_bytes(g_ref.at[c, 0], ag_send.at[c, 2])
+        else:
+            wait_bytes(g_ref.at[c, pl.ds(0, 3)], ag_send.at[c, 1])
 
     low_lanes = lax.broadcasted_iota(jnp.int32, (DH, 128), 1) < 64
 
@@ -227,66 +230,59 @@
             jnp.where(low_lanes, pltpu.roll(first, 64, 1), second),
         )
 
-    def attention(c):
+    def tiles():
         for yy in range(4):
             for hi in range(2):
-                if yy == 3 and hi == 1:
-                    continue
                 for m in range(2):
-                    tile = yy * 4 + hi * 2 + m
-                    for a in range(2):
-                        both = merge(
-                            g_ref[c, yy, 2 * m, hi, a].astype(F32), g_ref[c, yy, 2 * m + 1, hi, a].astype(F32)
-                        )
-                        for par in range(2):
-                            kvt[par, a, :, tile * 128 : tile * 128 + 128] = both[par].astype(BF16)
+                    if yy < 3 or hi == 0:
+                        yield yy, hi, m, slice((yy * 4 + hi * 2 + m) * 128, (yy * 4 + hi * 2 + m + 1) * 128)
+
+    def spread(c):
+        for yy, hi, m, lanes in tiles():
+            for a in range(2):
+                both = merge(g_ref[c, yy, 2 * m, hi, a].astype(F32), g_ref[c, yy, 2 * m + 1, hi, a].astype(F32))
+                for par in range(2):
+                    kvt[2 * c + par, a, :, lanes] = both[par].astype(BF16)
         for a in range(2):
             both = merge(r_ref[c, 0, a].astype(F32), r_ref[c, 1, a].astype(F32))
             for par in range(2):
-                qdt[par, a] = both[par].astype(BF16)
-
-        def one(par, carry):
-            query_t, grad_t = qdt[par, 0], qdt[par, 1]
-            query = query_t.astype(F32).T.astype(BF16)
-            grad = grad_t.astype(F32).T.astype(BF16)
-            keys_t, values_t = kvt[par, 0], kvt[par, 1]
-            s_ref[...] = dot(query, keys_t)
-            p_ref[...] = dot(grad, values_t)
-
-            def rows(g, inner):
-                at = pl.ds(pl.multiple_of(g * 16, 16), 16)
-                scores = s_ref[at] * (FACTOR * LOG2E) + bf[at]
-                top = jnp.max(scores, axis=1, keepdims=True)
-                exponent = jnp.exp2(scores - top)
-                slopes = p_ref[at]
-                total = jnp.sum(exponent, axis=1, keepdims=True)
-                mixed = jnp.sum(exponent * slopes, axis=1, keepdims=True)
-                inverse = 1.0 / total
-                weights = exponent * inverse
-                score_grad = weights * (slopes - mixed * inverse)
-                w_ref[at] = weights.astype(BF16)
-                ds_ref[at] = score_grad.astype(BF16)
+                qdt[2 * c + par, a] = both[par].astype(BF16)
+
+    def scores_of(s):
+        turned = [qdt[s, a].astype(F32).T.astype(BF16) for a in range(2)]
+        s_ref[s % 2] = dot(turned[0], kvt[s, 0])
+        p_ref[s % 2] = dot(turned[1], kvt[s, 1])
+
+    def softmax_of(s):
+        for g in range(8):
+            at = slice(g * 16, g * 16 + 16)
+            scores = s_ref[s % 2, at] * (FACTOR * LOG2E) + bf[at]
+            top = jnp.max(scores, axis=1, keepdims=True)
+            exponent = jnp.exp2(scores - top)
+            slopes = p_ref[s % 2, at]
+            total = jnp.sum(exponent, axis=1, keepdims=True)
+            mixed = jnp.sum(exponent * slopes, axis=1, keepdims=True)
+            inverse = 1.0 / total
+            weights = exponent * inverse
+            score_grad = weights * (slopes - mixed * inverse)
+            w_ref[s % 4, at] = weights.astype(BF16)
+            ds_ref[s % 4, at] = score_grad.astype(BF16)
+            if s:
                 db[at] += score_grad
-                return inner
-
-            lax.fori_loop(0, 8, rows, 0)
-            dkv[par, 0] = dot(query_t, ds_ref[...])
-            dkv[par, 1] = dot(grad_t, w_ref[...])
-            dq[par] = dot_nt(keys_t, ds_ref[...]) * FACTOR
-            return carry
-
-        lax.fori_loop(0, 2, one, 0)
-        for yy in range(4):
-            for hi in range(2):
-                if yy == 3 and hi == 1:
-                    continue
-                for m in range(2):
-                    tile = yy * 4 + hi * 2 + m
-                    for a in range(2):
-                        lanes = slice(tile * 128, tile * 128 + 128)
-                        both = merge(dkv[0, a, :, lanes], dkv[1, a, :, lanes])
-                        for e in range(2):
-                            d_ref[c, yy, 2 * m + e, hi, a] = both[e].astype(BF16)
+            else:
+                db[at] = score_grad
+
+    def grads_of(s):
+        dkv[s % 2, 0] = dot(qdt[s, 0], ds_ref[s % 4])
+        dkv[s % 2, 1] = dot(qdt[s, 1], w_ref[s % 4])
+        dq[s % 2] = dot_nt(kvt[s, 0], ds_ref[s % 4]) * FACTOR
+
+    def collect(c):
+        for yy, hi, m, lanes in tiles():
+            for a in range(2):
+                both = merge(dkv[0, a, :, lanes], dkv[1, a, :, lanes])
+                for e in range(2):
+                    d_ref[c, yy, 2 * m + e, hi, a] = both[e].astype(BF16)
         both = merge(dq[0], dq[1])
         for hi in range(2):
             qb[c, hi] = both[hi].astype(BF16)
@@ -363,48 +359,42 @@
         for i, ref in enumerate((h1, f1, h2, f2)):
             wait_bytes(ref.at[c], rs_send.at[c, i])
 
-    bias_rows(0)
     for c in range(CHUNKS):
         gather_1(c)
-    bias_rows(1)
-    for c in range(CHUNKS):
-        gather_2(c)
-    bias_rows(2)
-    for c in range(CHUNKS):
+    for c in range(2):
+        gather_2(c, (1, -1))
+    for c in range(2):
         gather_3(c)
-    bias_rows(3)
-    for c in range(CHUNKS):
-        gather_4(c)
+    for c in range(2, 4):
+        gather_2(c, (1, -1, 2))
 
     wait_bytes(r_ref, qd_sem.at[1])
     wait_bytes(br, bias_sem.at[1])
     mask = jnp.where(ac_ref[...] > 0, 0.0, -jnp.inf).astype(F32)
-
-    def widen(g, carry):
-        at = pl.ds(pl.multiple_of(g * 16, 16), 16)
+    for g in range(8):
+        at = slice(g * 16, g * 16 + 16)
         bf[at] = (br[at].astype(F32) + mask[:, :LIVE]) * LOG2E
-        return carry
-
-    lax.fori_loop(0, 8, widen, 0)
-
-    gather_5(0)
-    attention(0)
-    reduce_1(0)
-    query_back(0)
-    gather_5(1)
-    attention(1)
-    reduce_1(1)
-    reduce_2(0)
-    query_back(1)
-    gather_5(2)
-    attention(2)
-    reduce_1(2)
-    reduce_2(1)
-    reduce_3(0)
-    query_back(2)
-    gather_5(3)
-    attention(3)
-    reduce_1(3)
+
+    for c in range(2):
+        gather_4(c)
+        spread(c)
+        scores_of(2 * c)
+        scores_of(2 * c + 1)
+        softmax_of(2 * c)
+        grads_of(2 * c)
+        softmax_of(2 * c + 1)
+        grads_of(2 * c + 1)
+        collect(c)
+        reduce_1(c)
+        query_back(c)
+
+    for c in range(2, 4):
+        gather_4(c)
+        spread(c)
+        scores_of(2 * c)
+        scores_of(2 * c + 1)
+        softmax_of(2 * c)
+        softmax_of(2 * c + 1)
 
     for hi in range(2):
         for col in range(7):
@@ -421,19 +411,28 @@
             else:
                 pltpu.make_async_copy(src, dst, db_sem.at[1]).start()
 
+    reduce_2(0)
+    grads_of(4)
+    grads_of(5)
+    collect(2)
+    reduce_1(2)
+    reduce_2(1)
+    query_back(2)
+    grads_of(6)
+    grads_of(7)
+    collect(3)
+    reduce_1(3)
     query_back(3)
+    reduce_3(0)
+    reduce_3(1)
     reduce_2(2)
-    reduce_3(1)
     reduce_4(0)
     reduce_2(3)
-    reduce_3(2)
     reduce_4(1)
     reduce_5(0)
+    reduce_5(1)
+    reduce_3(2)
     reduce_3(3)
-    reduce_4(2)
-    reduce_5(1)
-    reduce_4(3)
-    reduce_5(2)
 
     @pl.when(live_cols)
     def _():
@@ -447,7 +446,7 @@
             left = jnp.concatenate([df[half, pl.ds(r, 16, stride=64)] for half in range(2)], axis=1)
             return acc + dot(left.astype(BF16), n_ref[r])
 
-        ra[y * 4 + x] = lax.fori_loop(0, 64, step, jnp.zeros((16, 128), F32))
+        ra[y * 4 + x] = lax.fori_loop(0, 64, step, jnp.zeros((16, 128), F32), unroll=8)
 
     @pl.when(cidx == 7)
     def _():
@@ -458,7 +457,8 @@
             if dy or dx:
                 mine = ra.at[y * 4 + x]
                 rcopy(mine, mine, ar_sem.at[0], ar_sem.at[1], dev(rem(x + dx, 4), rem(y + dy, 4), z, key)).start()
-    reduce_5(3)
+    reduce_4(2)
+    reduce_4(3)
     wait_bytes(ra.at[pl.ds(0, 15)], ar_sem.at[1])
     total = ra[0]
     for i in range(1, 16):
@@ -469,6 +469,8 @@
             mine = rb.at[head]
             rcopy(mine, mine, ar_sem.at[2], ar_sem.at[3], dev(x, y, zz, kk)).start()
 
+    reduce_5(2)
+    reduce_5(3)
     wait_bytes(ob, ob_sem.at[1])
     for a in range(3):
         o_ref[a] = ob[:, a].reshape(8 * DH, 128).astype(F32).T.astype(BF16)
@@ -478,7 +480,7 @@
     for i in range(1, 16):
         summed += rb[i]
     wg_ref[...] = summed * gain_ref[...]
-    gg_ref[...] = jnp.sum(summed * wt_ref[...], axis=0, keepdims=True)
+    gg_ref[...] = jnp.sum(summed * wt_ref[...].astype(F32), axis=0, keepdims=True)
 
     wait_bytes(skv.at[pl.ds(0, 7)], kv_send)
     wait_bytes(sqd.at[pl.ds(0, 7)], qd_sem.at[0])
@@ -512,12 +514,12 @@
         pltpu.VMEM((4, 16, 16, 256), BF16),
         pltpu.VMEM((ROWS, LIVE), BF16),
         pltpu.VMEM((ROWS, LIVE), F32),
-        pltpu.VMEM((2, 2, DH, LIVE), BF16),
-        pltpu.VMEM((2, 2, DH, 128), BF16),
-        pltpu.VMEM((ROWS, LIVE), F32),
-        pltpu.VMEM((ROWS, LIVE), F32),
-        pltpu.VMEM((ROWS, LIVE), BF16),
-        pltpu.VMEM((ROWS, LIVE), BF16),
+        pltpu.VMEM((8, 2, DH, LIVE), BF16),
+        pltpu.VMEM((8, 2, DH, 128), BF16),
+        pltpu.VMEM((2, ROWS, LIVE), F32),
+        pltpu.VMEM((2, ROWS, LIVE), F32),
+        pltpu.VMEM((4, ROWS, LIVE), BF16),
+        pltpu.VMEM((4, ROWS, LIVE), BF16),
         pltpu.VMEM((ROWS, LIVE), F32),
         pltpu.VMEM((2, 2, DH, LIVE), F32),
         pltpu.VMEM((2, DH, 128), F32),
@@ -539,7 +541,7 @@
         pltpu.SemaphoreType.DMA((4,)),
         pltpu.SemaphoreType.DMA((2,)),
         pltpu.SemaphoreType.DMA((2,)),
-        pltpu.SemaphoreType.DMA((4, 4)),
+        pltpu.SemaphoreType.DMA((4, 3)),
         pltpu.SemaphoreType.DMA((4, 4, 4, 2)),
         pltpu.SemaphoreType.DMA((4, 4)),
         pltpu.SemaphoreType.DMA((4, 8)),
@@ -571,7 +573,7 @@
     out, weight_t, gain_grad = fused(
         stacked,
         pair_feats,
-        bias_weight.astype(F32).T,
+        bias_weight.T,
         pair_gain[None],
         atom_counts[None],
     )

time: 115 us -> 92.4 us (0.80)
  Pallas kernels: 106 us -> 84.5 us
  other arithmetic: 3.03 us -> 1.75 us
    pallas_call x1, Pallas kernels: 106 us -> 84.5 us  [fused(): pl.pallas_call(kernel, out_shape=(jax.ShapeDtypeStruct((3, 128, 8 * DH),...]
    transpose x1 -> x0, other arithmetic: 1.29 us -> none  [local(): bias_weight.astype(F32)]
where the time goes in v2:
time: 92.4 us; the launch traced here: 92.2 us
  Pallas kernels  84.5 us (91%)
  local copies, waits for them, and re-layouts  5.35 us (6%)
  other arithmetic  1.75 us (2%)
    pallas_call x1, Pallas kernels, fused(): pl.pallas_call(kernel, out_shape=(jax.ShapeDtypeStruct((3, 128, 8 * DH),...  84.5 us
    unnamed x2, local copies, waits for them, and re-layouts  2.41 us

profile of v2, /device:TPU:1, one launch (start us, length us, event | category | flops | bytes accessed | tf_op | source)
XLA Modules:
  0.0 92.2 jit_solution(17720766754463884726)
XLA Ops:
  0.6 1.7 %maximum_bitcast_fusion = bf16[4,2,64,384]{3,1,2,0:T(2,128)(2,1)S(1)} fusion(bf16[1,64,2,384]{3,2,1,0:T(2,128)(2,1)} %bitcast.25, bf16[1,64,2,384]{3,2,1,0:T(2,128)(2,1)} %bitcast.26, bf16[1,64,2,384]{3,2,1,0:T(2,128)(2,1)} %bitcast.27, bf16[1,64,2,384]{3,2,1,0:T(2,128)(2,1)} %bitcast.28), kind=kLoop, calls=%fused_computation | loop fusion | flops 589824 | bytes 786432 | tf_op jit(solution)/shard_map/transpose | solution.py:572
  2.4 0.8 copy.13
  3.2 84.5 %shard_map.119 = (bf16[3,128,384]{2,1,0:T(8,128)(2,1)}, f32[16,128]{1,0:T(8,128)}, f32[1,128]{1,0:T(1,128)}) custom-call(bf16[4,128,384]{2,1,0:T(8,128)(2,1)} %bitcast.22, bf16[64,256,128]{2,1,0:T(8,128)(2,1)} %x_ref.1, bf16[16,128]{1,0:T(8,128)(2,1)} %bitcast.31, f32[1,128]{1,0:T(1,128)} %bitcast.32, s32[1,2048]{1,0:T(1,128)} %bitcast.29), custom_call_target="tpu_custom_call" | custom-call | tf_op jit(solution)/shard_map/pallas_call | solution.py:552
  87.7 1.3 %copy.16 = bf16[3,2,64,384]{3,1,2,0:T(2,128)(2,1)S(1)} copy(bf16[3,2,64,384]{3,2,1,0:T(8,128)(2,1)} %bitcast.24) | data formatting | bytes 589824 | tf_op jit(solution)/shard_map/reshape | solution.py:580
  88.9 0.9 slice_bitcast_fusion
  89.8 1.3 %copy.19 = f32[128,16]{0,1:T(8,128)} copy(f32[128,16]{0,1:T(8,128)} %bitcast.30) | data formatting | bytes 16384
  91.1 1.1 %copy.20 = f32[128]{0:T(128)} copy(f32[128]{0:T(128)} %bitcast.33) | data formatting | bytes 1024

commit v3 on v2

v3 whole, which is shorter than its diff:
```python
import jax
import jax.numpy as jnp
from jax import lax
from jax.experimental import pallas as pl
from jax.experimental.pallas import tpu as pltpu
from jax.sharding import PartitionSpec as P

DH = 48
HEADS = 16
TOKENS = 2048
LIVE = 1792
ROWS = 128
CHUNKS = 4
PAIRS = 14
FACTOR = DH ** (-0.5)
LOG2E = 1.4426950408889634
MESH = pl.DeviceIdType.MESH
F32 = jnp.float32
BF16 = jnp.bfloat16


def rem(a, b):
    return lax.rem(a, jnp.int32(b))


def div(a, b):
    return lax.div(a, jnp.int32(b))


def dot(a, b):
    return jnp.dot(a, b, preferred_element_type=F32)


def dot_nt(a, b):
    return lax.dot_general(a, b, (((1,), (1,)), ((), ())), preferred_element_type=F32)


def wait_bytes(ref, sem):
    pltpu.make_async_copy(ref, ref, sem).wait()


def kernel(
    ak_ref, av_ref, aq_ref, ag_ref, x_ref, wt_ref, gain_ref, ac_ref,
    o_ref, sum_ref,
    n_ref, skv, sqd, g_ref, r_ref, bsf, bs, br, bf,
    kvt, qdt, s_ref, p_ref, w_ref, ds_ref, db, dkv, dq, d_ref, qb,
    e_ref, f_ref, h_ref, fb, ob, dbs, dr, df, ra, rb,
    x_sem, kv_send, kv_recv, qd_sem, bias_sem, ag_send, ag_recv,
    rs_send, rs_recv, ob_sem, db_sem, ar_sem,
):
    smp = lax.axis_index("smp")
    qry = lax.axis_index("qry")
    key = lax.axis_index("key")
    y = div(qry, 8)
    zh = rem(div(qry, 4), 2)
    x = rem(qry, 4)
    z = zh * 4 + smp
    cidx = smp * 2 + key
    lx = rem(x, 2)
    vx = x - lx + key
    vx2 = rem(vx + 2, 4)
    sx = x - lx + 1 - key
    sx2 = rem(sx + 2, 4)
    head = lx * 8 + z
    same = key == lx
    live_cols = cidx < 7

    def dev(xx, yy, zz, kk):
        return (rem(zz, 4), yy * 8 + div(zz, 4) * 4 + xx, kk)

    def rcopy(src, dst, send, recv, device):
        return pltpu.make_async_remote_copy(
            src_ref=src, dst_ref=dst, send_sem=send, recv_sem=recv, device_id=device, device_id_type=MESH
        )

    def owner(zz, half):
        return dev(x - lx + half, y, zz, lx)

    def source(zz, kk):
        return dev(vx, y, zz, kk)

    def there(dx, dy):
        return dev(rem(x + dx, 4), rem(y + dy, 4), z, key)

    sibling = dev(x, y, z, 1 - key)

    def send(src, dst, sems, device, first):
        if not first:
            rcopy(src, dst, sems[0], sems[1], device).start()
            return

        @pl.when(same)
        def _():
            pltpu.make_async_copy(src, dst, sems[1]).start()

        @pl.when(jnp.logical_not(same))
        def _():
            rcopy(src, dst, sems[0], sems[1], device).start()

    x_copies = [
        pltpu.make_async_copy(x_ref.at[pl.ds(16 * rc, 16)], n_ref.at[pl.ds(16 * rc, 16)], x_sem.at[rc])
        for rc in range(4)
    ]
    for copy in x_copies:
        copy.start()

    barrier = pltpu.get_barrier_semaphore()
    near = []
    for dz in range(8):
        for dx in range(2):
            for dk in range(2):
                if dz or dx or dk:
                    near.append(dev(x - lx + rem(lx + dx, 2), y, rem(z + dz, 8), rem(key + dk, 2)))
    for dy in range(4):
        for dx in range(4):
            if dy or dx == 2:
                near.append(there(dx, dy))
    near.append(dev(rem(x + 3 - 2 * lx, 4), y, z, key))
    for device in near:
        pl.semaphore_signal(barrier, inc=1, device_id=device, device_id_type=MESH)

    a_refs = (ak_ref, av_ref, aq_ref, ag_ref)

    def turned(a):
        whole = a_refs[a][...].astype(F32)
        return jnp.concatenate([whole[:, i] for i in range(2)], axis=0).T.astype(BF16).reshape(8, DH, 128)

    for a in range(2):
        skv[:, a] = turned(a)

    gw = wt_ref[...].astype(F32) * gain_ref[...]
    gw_high = gw.astype(BF16)
    gw_low = (gw - gw_high.astype(F32)).astype(BF16)
    gw_both = jnp.concatenate([gw_high, gw_low], axis=0)

    def bias_rows(rc):
        x_copies[rc].wait()

        def step(i, carry):
            row = rc * 16 + 2 * i
            tile = n_ref[pl.ds(row, 2)].reshape(512, 128)
            wide = tile.astype(F32)
            center = wide - jnp.mean(wide, axis=1, keepdims=True)
            spread = jnp.mean(center * center, axis=1, keepdims=True)
            normed = (center * lax.rsqrt(spread + 1e-05)).astype(BF16)
            n_ref[pl.ds(row, 2)] = normed.reshape(2, 256, 128)
            out = dot_nt(gw_both, normed)
            out = out[:16] + out[16:]
            for j in range(2):
                for half in range(2):
                    bsf[half, pl.ds((2 * i + j) * 16, 16)] = out[:, j * 256 + half * 128 : j * 256 + half * 128 + 128]
            return carry

        lax.fori_loop(0, 8, step, 0, unroll=4)
        for h in range(16):
            pieces = [bsf[half, pl.ds(h, 16, stride=16)] for half in range(2)]
            bs[rc, h] = jnp.concatenate(pieces, axis=1).astype(BF16)

    def bias_send(rc):
        @pl.when(live_cols)
        def _():
            dst = br.at[pl.ds(zh * 64 + 16 * rc, 16), pl.ds(pl.multiple_of(cidx * 256, 256), 256)]
            for dz in range(8):
                for dk in range(2):
                    zz, half = rem(z + dz, 8), rem(lx + dk, 2)
                    src = bs.at[rc, half * 8 + zz]
                    send(src, dst, (bias_sem.at[0], bias_sem.at[1]), owner(zz, half), dz + dk == 0)

    bias_rows(0)
    pl.semaphore_wait(barrier, len(near))

    for dz in range(8):
        zz = rem(z + dz, 8)
        send(skv.at[zz], g_ref.at[smp, y, x, zh], (kv_send, kv_recv.at[smp]), owner(zz, key), dz == 0)

    bias_send(0)
    for c in range(CHUNKS):
        d_ref[c, 3, :, 1] = jnp.zeros((4, 2, DH, 128), BF16)
    bias_rows(1)
    bias_send(1)

    def gather_send(c, yy, xx, device):
        ref = g_ref.at[c, yy, xx]
        rcopy(ref, ref, ag_send.at[c], ag_recv.at[c, yy, xx], device).start()

    def gather_wait(c, yy, xx):
        wait_bytes(g_ref.at[c, yy, xx], ag_recv.at[c, yy, xx])

    lines = [rem(y + dy, 4) for dy in range(4)]

    def gather_1(c):
        wait_bytes(g_ref.at[c, y, vx], kv_recv.at[c])
        gather_send(c, y, vx, there(2, 0))
        for dy in (1, 3, 2):
            gather_send(c, y, vx, there(0, dy))
        gather_send(c, y, vx, sibling)

    def gather_2(c):
        if c % 2 == 0:
            gather_wait(c, y, vx2)
            for dy in (1, 3, 2):
                gather_send(c, y, vx2, there(0, dy))
            gather_send(c, y, vx2, sibling)
        else:
            for dy in (1, 3, 2):
                gather_wait(c, lines[dy], vx)
                gather_send(c, lines[dy], vx, there(2, 0))
                gather_send(c, lines[dy], vx, sibling)

    def gather_3(c):
        if c % 2 == 0:
            for dy in (1, 3, 2):
                for xx in (vx, vx2):
                    gather_wait(c, lines[dy], xx)
                    gather_send(c, lines[dy], xx, sibling)
        else:
            for dy in (0, 1, 3, 2):
                gather_wait(c, lines[dy], vx2)
                gather_send(c, lines[dy], vx2, sibling)

    def gather_4(c):
        for yy in range(4):
            for xx in (sx, sx2):
                gather_wait(c, yy, xx)

    low_lanes = lax.broadcasted_iota(jnp.int32, (DH, 128), 1) < 64

    def merge(first, second):
        return (
            jnp.where(low_lanes, first, pltpu.roll(second, 64, 1)),
            jnp.where(low_lanes, pltpu.roll(first, 64, 1), second),
        )

    def tiles():
        for yy in range(4):
            for hi in range(2):
                for m in range(2):
                    if yy < 3 or hi == 0:
                        yield yy, hi, m, slice((yy * 4 + hi * 2 + m) * 128, (yy * 4 + hi * 2 + m + 1) * 128)

    def spread(c):
        for yy, hi, m, lanes in tiles():
            for a in range(2):
                both = merge(g_ref[c, yy, 2 * m, hi, a].astype(F32), g_ref[c, yy, 2 * m + 1, hi, a].astype(F32))
                for par in range(2):
                    kvt[2 * c + par, a, :, lanes] = both[par].astype(BF16)
        for a in range(2):
            both = merge(r_ref[c, 0, a].astype(F32), r_ref[c, 1, a].astype(F32))
            for par in range(2):
                qdt[2 * c + par, a] = both[par].astype(BF16)

    def scores_of(s):
        turned = [qdt[s, a].astype(F32).T.astype(BF16) for a in range(2)]
        s_ref[s % 2] = dot(turned[0], kvt[s, 0])
        p_ref[s % 2] = dot(turned[1], kvt[s, 1])

    def softmax_of(s):
        for g in range(8):
            at = slice(g * 16, g * 16 + 16)
            scores = s_ref[s % 2, at] * (FACTOR * LOG2E) + bf[at]
            top = jnp.max(scores, axis=1, keepdims=True)
            exponent = jnp.exp2(scores - top)
            slopes = p_ref[s % 2, at]
            total = jnp.sum(exponent, axis=1, keepdims=True)
            mixed = jnp.sum(exponent * slopes, axis=1, keepdims=True)
            inverse = 1.0 / total
            weights = exponent * inverse
            score_grad = weights * (slopes - mixed * inverse)
            w_ref[s % 4, at] = weights.astype(BF16)
            ds_ref[s % 4, at] = score_grad.astype(BF16)
            if s:
                db[at] += score_grad
            else:
                db[at] = score_grad

    def grads_of(s):
        dkv[s % 2, 0] = dot(qdt[s, 0], ds_ref[s % 4])
        dkv[s % 2, 1] = dot(qdt[s, 1], w_ref[s % 4])
        dq[s % 2] = dot_nt(kvt[s, 0], ds_ref[s % 4]) * FACTOR

    def collect(c):
        for yy, hi, m, lanes in tiles():
            for a in range(2):
                both = merge(dkv[0, a, :, lanes], dkv[1, a, :, lanes])
                for e in range(2):
                    d_ref[c, yy, 2 * m + e, hi, a] = both[e].astype(BF16)
        both = merge(dq[0], dq[1])
        for hi in range(2):
            qb[c, hi] = both[hi].astype(BF16)

    def plus(ref, *others):
        total = ref[...].astype(F32)
        for other in others:
            total += other[...].astype(F32)
        return total

    def reduce_1(c):
        for j, xx in enumerate((sx, sx2)):
            rcopy(d_ref.at[c, :, xx], e_ref.at[c, j], rs_send.at[c, 0], rs_recv.at[c, 0], sibling).start()

    def reduce_2(c):
        wait_bytes(e_ref.at[c], rs_recv.at[c, 0])
        for j, xx in ((1, vx2), (0, vx)):
            for yy in range(4):
                ref = d_ref.at[c, yy, xx]
                ref[...] = plus(ref, e_ref.at[c, j, yy]).astype(BF16)
            if c % 2 and j:
                rcopy(d_ref.at[c, :, vx2], h_ref.at[c], rs_send.at[c, 1], rs_recv.at[c, 1], there(2, 0)).start()
        if c % 2 == 0:
            for dy in (2, 1, 3):
                for j, xx in enumerate((vx, vx2)):
                    rcopy(
                        d_ref.at[c, lines[dy], xx], f_ref.at[c, j, dy - 1],
                        rs_send.at[c, 1], rs_recv.at[c, 1], there(0, dy),
                    ).start()

    def reduce_3(c):
        if c % 2 == 0:
            wait_bytes(f_ref.at[c], rs_recv.at[c, 1])
            for j, xx in ((1, vx2), (0, vx)):
                ref = d_ref.at[c, y, xx]
                ref[...] = plus(ref, *(f_ref.at[c, j, i] for i in range(3))).astype(BF16)
                if j:
                    rcopy(ref, h_ref.at[c, 0], rs_send.at[c, 2], rs_recv.at[c, 2], there(2, 0)).start()
        else:
            wait_bytes(h_ref.at[c], rs_recv.at[c, 1])
            for dy in (2, 1, 3, 0):
                ref = d_ref.at[c, lines[dy], vx]
                ref[...] = plus(ref, h_ref.at[c, lines[dy]]).astype(BF16)
                if dy:
                    rcopy(
                        ref, f_ref.at[c, 0, dy - 1], rs_send.at[c, 2], rs_recv.at[c, 2], there(0, dy)
                    ).start()

    def reduce_4(c):
        if c % 2 == 0:
            wait_bytes(h_ref.at[c, 0], rs_recv.at[c, 2])
            others = [h_ref.at[c, 0]]
        else:
            wait_bytes(f_ref.at[c, 0], rs_recv.at[c, 2])
            others = [f_ref.at[c, 0, i] for i in range(3)]
        for hi in range(2):
            for a in range(2):
                total = plus(d_ref.at[c, y, vx, hi, a], *(other.at[hi, a] for other in others))
                fb[c, hi, a] = (total * FACTOR if a == 0 else total).astype(BF16)
            back(fb.at[c, hi], c, hi, 0, 2)

    def back(src, c, hi, lo, count):
        zz = jnp.int32(4 * hi + c)
        dst = ob.at[z, pl.ds(lo, count)]
        here = jnp.logical_and(same, zz == z)

        @pl.when(here)
        def _():
            pltpu.make_async_copy(src, dst, ob_sem.at[1]).start()

        @pl.when(jnp.logical_not(here))
        def _():
            rcopy(src, dst, ob_sem.at[0], ob_sem.at[1], source(zz, lx)).start()

    def query_back(c):
        for hi in range(2):
            back(qb.at[c, pl.ds(hi, 1)], c, hi, 2, 1)

    def reduce_end(c):
        sizes = (8, 6, 1) if c % 2 == 0 else (8, 4, 3)
        for i, size in enumerate(sizes):
            wait_bytes(blocks(size), rs_send.at[c, i])

    def blocks(count):
        return n_ref.at[pl.ds(0, 3 * count), pl.ds(0, 64)]

    for c in range(CHUNKS):
        gather_1(c)
    for a in range(2):
        sqd[:, a] = turned(2 + a)
    for dz in range(8):
        zz = rem(z + dz, 8)
        send(sqd.at[zz], r_ref.at[smp, zh], (qd_sem.at[0], qd_sem.at[1]), owner(zz, key), dz == 0)
    bias_rows(2)
    bias_send(2)
    for c in range(2):
        gather_2(c)
    bias_rows(3)
    bias_send(3)
    for c in range(2, CHUNKS):
        gather_2(c)
    for c in range(2):
        gather_3(c)

    wait_bytes(r_ref, qd_sem.at[1])
    wait_bytes(br, bias_sem.at[1])
    mask = jnp.where(ac_ref[...] > 0, 0.0, -jnp.inf).astype(F32)
    for g in range(8):
        at = slice(g * 16, g * 16 + 16)
        bf[at] = (br[at].astype(F32) + mask[:, :LIVE]) * LOG2E

    for c in range(2):
        gather_4(c)
        spread(c)
        scores_of(2 * c)
        scores_of(2 * c + 1)
        softmax_of(2 * c)
        grads_of(2 * c)
        softmax_of(2 * c + 1)
        grads_of(2 * c + 1)
        collect(c)
        reduce_1(c)
        query_back(c)
        gather_3(c + 2)

    for c in range(2, 4):
        gather_4(c)
        spread(c)
        scores_of(2 * c)
        scores_of(2 * c + 1)
        reduce_2(c - 2)
        softmax_of(2 * c)
        softmax_of(2 * c + 1)

    for hi in range(2):
        for col in range(7):
            dbs[hi * 8 + col] = db[hi * 64 : hi * 64 + 64, col * 256 : col * 256 + 256].astype(BF16)
    for dz in range(8):
        for dk in range(2):
            zz, kk = rem(z + dz, 8), rem(key + dk, 2)
            target = rem(zz, 4) * 2 + kk
            src = dbs.at[div(zz, 4) * 8 + target]

            @pl.when(target < 7)
            def _():
                send(src, dr.at[head], (db_sem.at[0], db_sem.at[1]), source(zz, kk), dz + dk == 0)

    grads_of(4)
    grads_of(5)
    collect(2)
    reduce_1(2)
    query_back(2)
    reduce_3(0)
    grads_of(6)
    grads_of(7)
    collect(3)
    reduce_1(3)
    query_back(3)
    reduce_3(1)
    reduce_2(2)
    reduce_2(3)
    reduce_4(0)
    reduce_4(1)
    reduce_3(2)
    reduce_3(3)

    @pl.when(live_cols)
    def _():
        wait_bytes(dr, db_sem.at[1])
        for h in range(16):
            wide = dr[h].astype(F32)
            for half in range(2):
                df[half, pl.ds(h * 64, 64)] = wide[:, half * 128 : half * 128 + 128]

        def step(r, acc):
            left = jnp.concatenate([df[half, pl.ds(r, 16, stride=64)] for half in range(2)], axis=1)
            return acc + dot(left.astype(BF16), n_ref[r])

        ra[y * 4 + x] = lax.fori_loop(0, 64, step, jnp.zeros((16, 128), F32), unroll=8)

    @pl.when(cidx == 7)
    def _():
        ra[y * 4 + x] = jnp.zeros((16, 128), F32)

    for dy in range(4):
        for dx in range(4):
            if dy or dx:
                mine = ra.at[y * 4 + x]
                rcopy(mine, mine, ar_sem.at[0], ar_sem.at[1], there(dx, dy)).start()
    reduce_4(2)
    reduce_4(3)
    wait_bytes(ra.at[pl.ds(0, 15)], ar_sem.at[1])
    total = ra[0]
    for i in range(1, 16):
        total += ra[i]
    mine = rb.at[key * 8 + z]
    mine[...] = total
    for dz in range(8):
        for dk in range(2):
            if dz or dk:
                rcopy(
                    mine, mine, ar_sem.at[2], ar_sem.at[3], dev(x, y, rem(z + dz, 8), rem(key + dk, 2))
                ).start()

    wait_bytes(ob, ob_sem.at[1])
    for a in range(3):
        o_ref[a] = ob[:, a].reshape(8 * DH, 128).astype(F32).T.astype(BF16)

    wait_bytes(rb.at[pl.ds(0, 15)], ar_sem.at[3])
    summed = rb[0]
    for i in range(1, 16):
        summed += rb[i]
    sum_ref[...] = summed

    def sent(count):
        wait_bytes(skv.at[pl.ds(0, count)], kv_send)
        wait_bytes(sqd.at[pl.ds(0, count)], qd_sem.at[0])
        wait_bytes(ob.at[pl.ds(0, count)], ob_sem.at[0])

        @pl.when(live_cols)
        def _():
            wait_bytes(bs.at[:, pl.ds(0, count + 8)], bias_sem.at[0])
            wait_bytes(dbs.at[pl.ds(0, count + 6)], db_sem.at[0])

        @pl.when(cidx == 7)
        def _():
            wait_bytes(dbs.at[pl.ds(0, 14)], db_sem.at[0])

    @pl.when(same)
    def _():
        sent(7)

    @pl.when(jnp.logical_not(same))
    def _():
        sent(8)

    for c in range(CHUNKS):
        wait_bytes(blocks(15), ag_send.at[c])
        reduce_end(c)
    wait_bytes(ra.at[pl.ds(0, 15)], ar_sem.at[0])
    wait_bytes(rb.at[pl.ds(0, 15)], ar_sem.at[2])


def fused(rows, pair_feats, weight_t, gain, counts):
    vmem = pl.BlockSpec(memory_space=pltpu.VMEM)
    scratch = [
        pltpu.VMEM((64, 256, 128), BF16),
        pltpu.VMEM((8, 2, DH, 128), BF16),
        pltpu.VMEM((8, 2, DH, 128), BF16),
        pltpu.VMEM((4, 4, 4, 2, 2, DH, 128), BF16),
        pltpu.VMEM((4, 2, 2, DH, 128), BF16),
        pltpu.VMEM((2, 256, 128), F32),
        pltpu.VMEM((4, 16, 16, 256), BF16),
        pltpu.VMEM((ROWS, LIVE), BF16),
        pltpu.VMEM((ROWS, LIVE), F32),
        pltpu.VMEM((8, 2, DH, LIVE), BF16),
        pltpu.VMEM((8, 2, DH, 128), BF16),
        pltpu.VMEM((2, ROWS, LIVE), F32),
        pltpu.VMEM((2, ROWS, LIVE), F32),
        pltpu.VMEM((4, ROWS, LIVE), BF16),
        pltpu.VMEM((4, ROWS, LIVE), BF16),
        pltpu.VMEM((ROWS, LIVE), F32),
        pltpu.VMEM((2, 2, DH, LIVE), F32),
        pltpu.VMEM((2, DH, 128), F32),
        pltpu.VMEM((4, 4, 4, 2, 2, DH, 128), BF16),
        pltpu.VMEM((4, 2, DH, 128), BF16),
        pltpu.VMEM((4, 2, 4, 2, 2, DH, 128), BF16),
        pltpu.VMEM((4, 2, 3, 2, 2, DH, 128), BF16),
        pltpu.VMEM((4, 4, 2, 2, DH, 128), BF16),
        pltpu.VMEM((4, 2, 2, DH, 128), BF16),
        pltpu.VMEM((8, 3, DH, 128), BF16),
        pltpu.VMEM((16, 64, 256), BF16),
        pltpu.VMEM((16, 64, 256), BF16),
        pltpu.VMEM((2, 1024, 128), F32),
        pltpu.VMEM((16, 16, 128), F32),
        pltpu.VMEM((16, 16, 128), F32),
        pltpu.SemaphoreType.DMA((4,)),
        pltpu.SemaphoreType.DMA,
        pltpu.SemaphoreType.DMA((4,)),
        pltpu.SemaphoreType.DMA((2,)),
        pltpu.SemaphoreType.DMA((2,)),
        pltpu.SemaphoreType.DMA((4,)),
        pltpu.SemaphoreType.DMA((4, 4, 4)),
        pltpu.SemaphoreType.DMA((4, 3)),
        pltpu.SemaphoreType.DMA((4, 3)),
        pltpu.SemaphoreType.DMA((2,)),
        pltpu.SemaphoreType.DMA((2,)),
        pltpu.SemaphoreType.DMA((4,)),
    ]
    return pl.pallas_call(
        kernel,
        out_shape=(
            jax.ShapeDtypeStruct((3, 128, 8 * DH), BF16),
            jax.ShapeDtypeStruct((16, 128), F32),
        ),
        in_specs=[vmem, vmem, vmem, vmem, pl.BlockSpec(memory_space=pl.ANY), vmem, vmem, vmem],
        out_specs=(vmem, vmem),
        scratch_shapes=scratch,
        compiler_params=pltpu.CompilerParams(
            collective_id=0, has_side_effects=True, vmem_limit_bytes=56 * 1024 * 1024
        ),
    )(*rows, pair_feats, weight_t, gain, counts)


def finish(o_ref, sum_ref, wt_ref, gain_ref, key_ref, value_ref, query_ref, wg_ref, gg_ref):
    for a, ref in enumerate((key_ref, value_ref, query_ref)):
        whole = o_ref[a].astype(F32)
        ref[...] = jnp.stack([whole[:64], whole[64:]], axis=1).astype(BF16)
    summed = sum_ref[...]
    wg_ref[...] = summed * gain_ref[...]
    gg_ref[...] = jnp.sum(summed * wt_ref[...].astype(F32), axis=0, keepdims=True)


def local(
    query_proj, key_proj, value_proj, grad_out, pair_feats, pair_gain, bias_weight, atom_counts
):
    gain, weight_t = pair_gain[None], bias_weight.T
    out, summed = fused(
        (key_proj, value_proj, query_proj, grad_out), pair_feats, weight_t, gain, atom_counts[None]
    )
    vmem = pl.BlockSpec(memory_space=pltpu.VMEM)
    tokens = jax.ShapeDtypeStruct(query_proj.shape, BF16)
    key_grad, value_grad, query_grad, weight_grad, gain_grad = pl.pallas_call(
        finish,
        out_shape=(
            tokens,
            tokens,
            tokens,
            jax.ShapeDtypeStruct((16, 128), F32),
            jax.ShapeDtypeStruct((1, 128), F32),
        ),
        in_specs=[vmem] * 4,
        out_specs=(vmem,) * 5,
    )(out, summed, weight_t, gain)
    return query_grad, key_grad, value_grad, weight_grad.T, gain_grad[0]


def solution(mesh):
    tokens = P("qry", "smp", "key")
    return jax.shard_map(
        local,
        mesh=mesh,
        in_specs=(tokens, tokens, tokens, tokens, P("qry", ("smp", "key"), None), P(), P(), P()),
        out_specs=(tokens, tokens, tokens, P(), P()),
        check_vma=False,
    )
```

time: 92.4 us -> 81.7 us (0.88)
  local copies, waits for them, and re-layouts: 5.35 us -> 0 us
  Pallas kernels: 84.5 us -> 80.9 us
  other arithmetic: 1.75 us -> 0 us
    pallas_call x1, Pallas kernels: 84.5 us -> 78.8 us  [fused(): pl.pallas_call(kernel, out_shape=(jax.ShapeDtypeStruct((3, 128, 8 * DH),...]
    unnamed x2 -> x0, local copies, waits for them, and re-layouts: 2.41 us -> none
    pallas_call x0 -> x1, Pallas kernels: none -> 2.13 us  [local(): pl.pallas_call(finish, out_shape=(tokens, tokens, tokens, jax.ShapeDtypeS...]
    transpose x1 -> x0, other arithmetic: 1.75 us -> none  [local(): stacked = stacked.transpose(0, 2, 1, 3).reshape(4, 128, 8 * DH)]
    reshape x1 -> x0, local copies, waits for them, and re-layouts: 1.27 us -> none  [local(): out = out.reshape(3, 2, 64, 8 * DH).transpose(0, 2, 1, 3)]
where the time goes in v3:
time: 81.7 us; the launch traced here: 81.5 us
  Pallas kernels  80.9 us (99%)
    pallas_call x1, Pallas kernels, fused(): pl.pallas_call(kernel, out_shape=(jax.ShapeDtypeStruct((3, 128, 8 * DH),...  78.8 us
    pallas_call x1, Pallas kernels, local(): pl.pallas_call(finish, out_shape=(tokens, tokens, tokens, jax.ShapeDtypeS...  2.13 us

profile of v3, /device:TPU:1, one launch (start us, length us, event | category | flops | bytes accessed | tf_op | source)
XLA Modules:
  0.0 81.5 jit_solution(6493453383160740199)
XLA Ops:
  0.6 78.8 %shard_map.119 = (bf16[3,128,384]{2,1,0:T(8,128)(2,1)}, f32[16,128]{1,0:T(8,128)}) custom-call(bf16[64,2,384]{2,1,0:T(2,128)(2,1)} %ak_ref.1, bf16[64,2,384]{2,1,0:T(2,128)(2,1)} %av_ref.1, bf16[64,2,384]{2,1,0:T(2,128)(2,1)} %aq_ref.1, bf16[64,2,384]{2,1,0:T(2,128)(2,1)} %ag_ref.1, bf16[64,256,128]{2,1,0:T(8,128)(2,1)} %x_ref.1, bf16[16,128]{1,0:T(8,128)(2,1)} %bitcast.5, ...), custom_call_target="tpu_custom_call" | custom-call | tf_op jit(solution)/shard_map/pallas_call | solution.py:576
  79.4 2.1 %shard_map.120 = (bf16[64,2,384]{2,1,0:T(2,128)(2,1)}, bf16[64,2,384]{2,1,0:T(2,128)(2,1)}, bf16[64,2,384]{2,1,0:T(2,128)(2,1)}, f32[16,128]{1,0:T(8,128)}, f32[1,128]{1,0:T(1,128)}) custom-call(bf16[3,128,384]{2,1,0:T(8,128)(2,1)} %get-tuple-element.12.o_ref, f32[16,128]{1,0:T(8,128)} %get-tuple-element.13.sum_ref, bf16[16,128]{1,0:T(8,128)(2,1)} %bitcast.6, ...), custom_call_target="tpu_custom_call" | custom-call | tf_op jit(solution)/shard_map/pallas_call | solution.py:609

commit v4 on v3

--- a/solution.py
+++ b/solution.py
@@ -266,17 +266,17 @@
             inverse = 1.0 / total
             weights = exponent * inverse
             score_grad = weights * (slopes - mixed * inverse)
-            w_ref[s % 4, at] = weights.astype(BF16)
-            ds_ref[s % 4, at] = score_grad.astype(BF16)
+            w_ref[s, at] = weights.astype(BF16)
+            ds_ref[s, at] = score_grad.astype(BF16)
             if s:
                 db[at] += score_grad
             else:
                 db[at] = score_grad
 
     def grads_of(s):
-        dkv[s % 2, 0] = dot(qdt[s, 0], ds_ref[s % 4])
-        dkv[s % 2, 1] = dot(qdt[s, 1], w_ref[s % 4])
-        dq[s % 2] = dot_nt(kvt[s, 0], ds_ref[s % 4]) * FACTOR
+        dkv[s % 2, 0] = dot(qdt[s, 0], ds_ref[s])
+        dkv[s % 2, 1] = dot(qdt[s, 1], w_ref[s])
+        dq[s % 2] = dot_nt(kvt[s, 0], ds_ref[s]) * FACTOR
 
     def collect(c):
         for yy, hi, m, lanes in tiles():
@@ -304,9 +304,9 @@
             for yy in range(4):
                 ref = d_ref.at[c, yy, xx]
                 ref[...] = plus(ref, e_ref.at[c, j, yy]).astype(BF16)
-            if c % 2 and j:
+            if False and j:
                 rcopy(d_ref.at[c, :, vx2], h_ref.at[c], rs_send.at[c, 1], rs_recv.at[c, 1], there(2, 0)).start()
-        if c % 2 == 0:
+        if True:
             for dy in (2, 1, 3):
                 for j, xx in enumerate((vx, vx2)):
                     rcopy(
@@ -315,7 +315,7 @@
                     ).start()
 
     def reduce_3(c):
-        if c % 2 == 0:
+        if True:
             wait_bytes(f_ref.at[c], rs_recv.at[c, 1])
             for j, xx in ((1, vx2), (0, vx)):
                 ref = d_ref.at[c, y, xx]
@@ -333,7 +333,7 @@
                     ).start()
 
     def reduce_4(c):
-        if c % 2 == 0:
+        if True:
             wait_bytes(h_ref.at[c, 0], rs_recv.at[c, 2])
             others = [h_ref.at[c, 0]]
         else:
@@ -363,7 +363,7 @@
             back(qb.at[c, pl.ds(hi, 1)], c, hi, 2, 1)
 
     def reduce_end(c):
-        sizes = (8, 6, 1) if c % 2 == 0 else (8, 4, 3)
+        sizes = (8, 6, 1) if True else (8, 4, 3)
         for i, size in enumerate(sizes):
             wait_bytes(blocks(size), rs_send.at[c, i])
 
@@ -395,28 +395,29 @@
         at = slice(g * 16, g * 16 + 16)
         bf[at] = (br[at].astype(F32) + mask[:, :LIVE]) * LOG2E
 
-    for c in range(2):
+    def forward(c):
         gather_4(c)
         spread(c)
         scores_of(2 * c)
         scores_of(2 * c + 1)
         softmax_of(2 * c)
+        softmax_of(2 * c + 1)
+
+    def backward(c):
         grads_of(2 * c)
-        softmax_of(2 * c + 1)
         grads_of(2 * c + 1)
         collect(c)
         reduce_1(c)
-        query_back(c)
-        gather_3(c + 2)
-
-    for c in range(2, 4):
-        gather_4(c)
-        spread(c)
-        scores_of(2 * c)
-        scores_of(2 * c + 1)
-        reduce_2(c - 2)
-        softmax_of(2 * c)
-        softmax_of(2 * c + 1)
+
+    forward(0)
+    gather_3(2)
+    backward(0)
+    query_back(0)
+    forward(1)
+    gather_3(3)
+    reduce_2(0)
+    forward(2)
+    forward(3)
 
     for hi in range(2):
         for col in range(7):
@@ -431,24 +432,20 @@
             def _():
                 send(src, dr.at[head], (db_sem.at[0], db_sem.at[1]), source(zz, kk), dz + dk == 0)
 
-    grads_of(4)
-    grads_of(5)
-    collect(2)
-    reduce_1(2)
+    backward(1)
+    reduce_3(0)
+    query_back(1)
+    backward(2)
+    reduce_2(1)
     query_back(2)
-    reduce_3(0)
-    grads_of(6)
-    grads_of(7)
-    collect(3)
-    reduce_1(3)
+    backward(3)
+    reduce_2(2)
+    reduce_4(0)
+    reduce_3(1)
+    reduce_2(3)
     query_back(3)
-    reduce_3(1)
-    reduce_2(2)
-    reduce_2(3)
-    reduce_4(0)
+    reduce_3(2)
     reduce_4(1)
-    reduce_3(2)
-    reduce_3(3)
 
     @pl.when(live_cols)
     def _():
@@ -462,31 +459,32 @@
             left = jnp.concatenate([df[half, pl.ds(r, 16, stride=64)] for half in range(2)], axis=1)
             return acc + dot(left.astype(BF16), n_ref[r])
 
-        ra[y * 4 + x] = lax.fori_loop(0, 64, step, jnp.zeros((16, 128), F32), unroll=8)
+        ra[key * 8 + z] = lax.fori_loop(0, 64, step, jnp.zeros((16, 128), F32), unroll=8)
 
     @pl.when(cidx == 7)
     def _():
-        ra[y * 4 + x] = jnp.zeros((16, 128), F32)
-
-    for dy in range(4):
-        for dx in range(4):
-            if dy or dx:
-                mine = ra.at[y * 4 + x]
-                rcopy(mine, mine, ar_sem.at[0], ar_sem.at[1], there(dx, dy)).start()
+        ra[key * 8 + z] = jnp.zeros((16, 128), F32)
+
+    mine = ra.at[key * 8 + z]
+    for dz in range(8):
+        for dk in range(2):
+            if dz or dk:
+                rcopy(
+                    mine, mine, ar_sem.at[0], ar_sem.at[1], dev(x, y, rem(z + dz, 8), rem(key + dk, 2))
+                ).start()
+    reduce_3(3)
     reduce_4(2)
     reduce_4(3)
     wait_bytes(ra.at[pl.ds(0, 15)], ar_sem.at[1])
     total = ra[0]
     for i in range(1, 16):
         total += ra[i]
-    mine = rb.at[key * 8 + z]
-    mine[...] = total
-    for dz in range(8):
-        for dk in range(2):
-            if dz or dk:
-                rcopy(
-                    mine, mine, ar_sem.at[2], ar_sem.at[3], dev(x, y, rem(z + dz, 8), rem(key + dk, 2))
-                ).start()
+    last = rb.at[y * 4 + x]
+    last[...] = total
+    for dy in range(4):
+        for dx in range(4):
+            if dy or dx:
+                rcopy(last, last, ar_sem.at[2], ar_sem.at[3], there(dx, dy)).start()
 
     wait_bytes(ob, ob_sem.at[1])
     for a in range(3):
@@ -543,8 +541,8 @@
         pltpu.VMEM((8, 2, DH, 128), BF16),
         pltpu.VMEM((2, ROWS, LIVE), F32),
         pltpu.VMEM((2, ROWS, LIVE), F32),
-        pltpu.VMEM((4, ROWS, LIVE), BF16),
-        pltpu.VMEM((4, ROWS, LIVE), BF16),
+        pltpu.VMEM((8, ROWS, LIVE), BF16),
+        pltpu.VMEM((8, ROWS, LIVE), BF16),
         pltpu.VMEM((ROWS, LIVE), F32),
         pltpu.VMEM((2, 2, DH, LIVE), F32),
         pltpu.VMEM((2, DH, 128), F32),

time: 81.7 us -> 78 us (0.955)
  Pallas kernels: 80.9 us -> 77.3 us
    pallas_call x1, Pallas kernels: 78.8 us -> 75.1 us  [fused(): pl.pallas_call(kernel, out_shape=(jax.ShapeDtypeStruct((3, 128, 8 * DH),...]
where the time goes in v4:
time: 78 us; the launch traced here: 77.9 us
  Pallas kernels  77.3 us (99%)
    pallas_call x1, Pallas kernels, fused(): pl.pallas_call(kernel, out_shape=(jax.ShapeDtypeStruct((3, 128, 8 * DH),...  75.1 us
    pallas_call x1, Pallas kernels, local(): pl.pallas_call(finish, out_shape=(tokens, tokens, tokens, jax.ShapeDtypeS...  2.13 us

profile of v4, /device:TPU:1, one launch (start us, length us, event | category | flops | bytes accessed | tf_op | source)
XLA Modules:
  0.0 77.9 jit_solution(7565831436116854883)
XLA Ops:
  0.6 75.1 %shard_map.119 = (bf16[3,128,384]{2,1,0:T(8,128)(2,1)}, f32[16,128]{1,0:T(8,128)}) custom-call(bf16[64,2,384]{2,1,0:T(2,128)(2,1)} %ak_ref.1, bf16[64,2,384]{2,1,0:T(2,128)(2,1)} %av_ref.1, bf16[64,2,384]{2,1,0:T(2,128)(2,1)} %aq_ref.1, bf16[64,2,384]{2,1,0:T(2,128)(2,1)} %ag_ref.1, bf16[64,256,128]{2,1,0:T(8,128)(2,1)} %x_ref.1, bf16[16,128]{1,0:T(8,128)(2,1)} %bitcast.5, ...), custom_call_target="tpu_custom_call" | custom-call | tf_op jit(solution)/shard_map/pallas_call | solution.py:574
  75.8 2.1 %shard_map.120 = (bf16[64,2,384]{2,1,0:T(2,128)(2,1)}, bf16[64,2,384]{2,1,0:T(2,128)(2,1)}, bf16[64,2,384]{2,1,0:T(2,128)(2,1)}, f32[16,128]{1,0:T(8,128)}, f32[1,128]{1,0:T(1,128)}) custom-call(bf16[3,128,384]{2,1,0:T(8,128)(2,1)} %get-tuple-element.12.o_ref, f32[16,128]{1,0:T(8,128)} %get-tuple-element.13.sum_ref, bf16[16,128]{1,0:T(8,128)(2,1)} %bitcast.6, ...), custom_call_target="tpu_custom_call" | custom-call | tf_op jit(solution)/shard_map/pallas_call | solution.py:607

commit v5 on v4

--- a/solution.py
+++ b/solution.py
@@ -444,8 +444,6 @@
     reduce_3(1)
     reduce_2(3)
     query_back(3)
-    reduce_3(2)
-    reduce_4(1)
 
     @pl.when(live_cols)
     def _():
@@ -472,7 +470,9 @@
                 rcopy(
                     mine, mine, ar_sem.at[0], ar_sem.at[1], dev(x, y, rem(z + dz, 8), rem(key + dk, 2))
                 ).start()
+    reduce_3(2)
     reduce_3(3)
+    reduce_4(1)
     reduce_4(2)
     reduce_4(3)
     wait_bytes(ra.at[pl.ds(0, 15)], ar_sem.at[1])

time: 78 us -> 75.6 us (0.969)
  Pallas kernels: 77.3 us -> 74.5 us
    pallas_call x1, Pallas kernels: 75.1 us -> 72.4 us  [fused(): pl.pallas_call(kernel, out_shape=(jax.ShapeDtypeStruct((3, 128, 8 * DH),...]
where the time goes in v5:
time: 75.6 us; the launch traced here: 75.2 us
  Pallas kernels  74.5 us (99%)
    pallas_call x1, Pallas kernels, fused(): pl.pallas_call(kernel, out_shape=(jax.ShapeDtypeStruct((3, 128, 8 * DH),...  72.4 us
    pallas_call x1, Pallas kernels, local(): pl.pallas_call(finish, out_shape=(tokens, tokens, tokens, jax.ShapeDtypeS...  2.13 us

profile of v5, /device:TPU:1, one launch (start us, length us, event | category | flops | bytes accessed | tf_op | source)
XLA Modules:
  0.0 75.2 jit_solution(10354381053833350033)
XLA Ops:
  0.6 72.4 %shard_map.119 = (bf16[3,128,384]{2,1,0:T(8,128)(2,1)}, f32[16,128]{1,0:T(8,128)}) custom-call(bf16[64,2,384]{2,1,0:T(2,128)(2,1)} %ak_ref.1, bf16[64,2,384]{2,1,0:T(2,128)(2,1)} %av_ref.1, bf16[64,2,384]{2,1,0:T(2,128)(2,1)} %aq_ref.1, bf16[64,2,384]{2,1,0:T(2,128)(2,1)} %ag_ref.1, bf16[64,256,128]{2,1,0:T(8,128)(2,1)} %x_ref.1, bf16[16,128]{1,0:T(8,128)(2,1)} %bitcast.5, ...), custom_call_target="tpu_custom_call" | custom-call | tf_op jit(solution)/shard_map/pallas_call | solution.py:574
  73.0 2.1 %shard_map.120 = (bf16[64,2,384]{2,1,0:T(2,128)(2,1)}, bf16[64,2,384]{2,1,0:T(2,128)(2,1)}, bf16[64,2,384]{2,1,0:T(2,128)(2,1)}, f32[16,128]{1,0:T(8,128)}, f32[1,128]{1,0:T(1,128)}) custom-call(bf16[3,128,384]{2,1,0:T(8,128)(2,1)} %get-tuple-element.12.o_ref, f32[16,128]{1,0:T(8,128)} %get-tuple-element.13.sum_ref, bf16[16,128]{1,0:T(8,128)(2,1)} %bitcast.6, ...), custom_call_target="tpu_custom_call" | custom-call | tf_op jit(solution)/shard_map/pallas_call | solution.py:607
